TPU v7x, 32 devices: a whole 2x2x4 slice. The times are simulated.
32 devices in a mesh: sub: 32 (over z, y, x, core).
Axes of the slice: x: 2, y: 2, z: 4, core: 2. Of those that a mesh axis runs over, the one named last changes fastest.
Arguments:
- stiffness: bfloat16 [32, 1536, 1536], P('sub'), may hold values from -2 to 5, as said below
- local_inverse: bfloat16 [32, 1536, 1536], P('sub'), may hold values from -0.2 to 0.5, as said below
- coarse_basis: float32 [32, 48, 1536], P('sub'), may hold values from -0.15625 to 0.15625
- loads: float32 [32, 1536, 128], P('sub'), may hold values from -8 to 8
- counts: int32 [32, 1536], P('sub'), may hold values from 1 to 2, as said below
- shared_rows: int32 [32, 4, 256], P('sub'), may hold values from 0 to 1536, as said below
- coarse_map: int32 [32, 48], P('sub'), may hold values from 0 to 4095
- coarse_inverse: float32 [4096, 4096], P('sub'), may hold values from -1 to 2, as said below
Outputs:
- solution: float32 [32, 1536, 128], P('sub')
- residual: float32 [32, 1536, 128], P('sub')
Inputs may be any that keep to these rules, and one draw needn't show every extreme that they name: `shared_rows`: for k = 0..3 entry [s, k, t] names a row of subdomain s shared with its slot-k neighbour, or 1536 where unused; live entries come first; entry t of s's list for a neighbour and entry t of that neighbour's list for s name the same unknown; no row appears in two lists of one subdomain; some pair of each kind has exactly 256 live entries. `counts`: 1 plus the number of lists of its subdomain that name the row. `stiffness`: Symmetric. `local_inverse`: Symmetric. `coarse_inverse`: Symmetric. `coarse_map`: A subdomain may name a coarse unknown more than once.
All inputs are finite; a program needn't handle non-finite values.
Results may differ from a plain program's by a relative error of at most 0.0081.
Values sent between devices are 32-bit elements; how exact they have to be, the bound alone decides.
No kernel may reach another device: no remote copies, remote signals or barrier semaphores. Data moves between devices by JAX's collectives and lax.ppermute only.
A program may use at most 128 MiB of HBM per device.

v0:
```python
import jax
import jax.numpy as jnp
from jax import lax
from jax.sharding import PartitionSpec as P

STRIDE = 8
ITERS = 3


highest = lax.Precision.HIGHEST
opposite_slot = (1, 0, 3, 2)


def shifted(block, axis, distance):
    devices = range(lax.axis_size(axis))
    route = [((i - distance) % len(devices), i) for i in devices]
    return lax.ppermute(block, axis, route)


def assemble(local, row_lists):
    assembled = local
    for slot_index, offset in enumerate((1, -1, STRIDE, -STRIDE)):
        outgoing = jnp.take(local, row_lists[slot_index], axis=0, mode="fill", fill_value=0.0)
        arrived = shifted(outgoing, "sub", offset)
        assembled = assembled.at[row_lists[opposite_slot[slot_index]]].add(arrived, mode="drop")
    return assembled


def body(
    stiffness, local_inverse, coarse_basis, loads, counts, shared_rows, coarse_map, coarse_inverse
):
    schur_block = stiffness[0]
    inverse_block = local_inverse[0]
    basis_block = coarse_basis[0]
    row_lists = shared_rows[0]
    coarse_ids = coarse_map[0]
    weights = 1.0 / counts[0].astype(jnp.float32)
    coarse_order = coarse_inverse.shape[1]

    def precond(resid):
        scaled = resid * weights[:, None]
        local_part = jnp.dot(
            inverse_block, scaled.astype(jnp.bfloat16), preferred_element_type=jnp.float32
        )
        coarse_terms = jnp.dot(basis_block, scaled, precision=highest)
        placed = (
            jnp.zeros((coarse_order, coarse_terms.shape[1]), jnp.float32)
            .at[coarse_ids]
            .add(coarse_terms)
        )
        merged_norm = False
        full_total = lax.psum(placed, "sub")
        owned_values = jnp.dot(coarse_inverse, full_total, precision=highest)
        coarse_values = lax.all_gather(owned_values, "sub", axis=0, tiled=True)
        picked = coarse_values[coarse_ids]
        back = jnp.dot(basis_block.T, picked, precision=highest)
        result = assemble(weights[:, None] * (local_part + back), row_lists)
        norm_value = lax.psum(jnp.sum(weights[:, None] * resid * result, axis=0), "sub")
        return (result, norm_value)

    residual = assemble(loads[0], row_lists)
    solution = jnp.zeros_like(residual)
    precond_now, norm_now = precond(residual)
    direction = precond_now
    for iteration in range(ITERS):
        local_image = jnp.dot(
            schur_block, direction.astype(jnp.bfloat16), preferred_element_type=jnp.float32
        )
        image = assemble(local_image, row_lists)
        energy = lax.psum(jnp.sum(weights[:, None] * direction * image, axis=0), "sub")
        alpha = norm_now / energy
        solution = solution + alpha * direction
        residual = residual - alpha * image
        if iteration + 1 < ITERS:
            precond_now, norm_next = precond(residual)
            direction = precond_now + norm_next / norm_now * direction
            norm_now = norm_next
    return (solution[None], residual[None])


def solution(mesh):
    placed = (
        P("sub", None, None),
        P("sub", None, None),
        P("sub", None, None),
        P("sub", None, None),
        P("sub", None),
        P("sub", None, None),
        P("sub", None),
        P("sub", None),
    )
    return jax.shard_map(
        body,
        mesh=mesh,
        in_specs=placed,
        out_specs=(P("sub", None, None), P("sub", None, None)),
        check_vma=False,
    )
```

profile of v0, /device:TPU:0, one launch (start us, length us, event | category | flops | bytes accessed | tf_op | source)
XLA Modules:
  0.0 1098.4 jit_solution(7425300774299160202)
XLA Ops:
  12.9 5.9 collective-permute-start.1
  38.0 130.2 %all-reduce.5.cloned.1.call-done = f32[4096,128]{1,0:T(8,128)} async-done(((f32[4096,128]{1,0:T(8,128)}), f32[4096,128]{1,0:T(8,128)}) %all-reduce.5.cloned.1.call-update) | async-done | bytes 2097168 | tf_op jit(solution)/shard_map/psum | solution.py:52
  173.0 55.1 %all-gather.4.cloned.1.call-done = f32[4096,128]{1,0:T(8,128)} async-done(((f32[128,128]{1,0:T(8,128)}), f32[4096,128]{1,0:T(8,128)}) %all-gather.4.cloned.1.call-update) | async-done | bytes 2097168 | tf_op jit(solution)/shard_map/all_gather | solution.py:54
  231.1 5.2 fusion.35
  250.3 5.1 collective-permute-start.5
  276.5 5.1 fusion.26
  295.3 5.3 collective-permute-start.9
  323.8 36.9 %all-reduce = (f32[128]{0:T(128)S(1)}, f32[128]{0:T(128)S(1)}) all-reduce(f32[128]{0:T(128)S(1)} %get-tuple-element.4, f32[128]{0:T(128)S(1)} %get-tuple-element.3), channel_id=1, replica_groups=mesh['sub'=32] {'sub'}, use_global_device_ids=true, to_apply=%region_11.13 | all-reduce | flops 256 | bytes 2048 | tf_op jit(solution)/shard_map/psum | solution.py:58
  365.8 134.3 %all-reduce.7.cloned.1.call-done = f32[4096,128]{1,0:T(8,128)} async-done(((f32[4096,128]{1,0:T(8,128)}), f32[4096,128]{1,0:T(8,128)}) %all-reduce.7.cloned.1.call-update) | async-done | bytes 2097168 | tf_op jit(solution)/shard_map/psum | solution.py:52
  504.6 55.4 %all-gather.6.cloned.1.call-done = f32[4096,128]{1,0:T(8,128)} async-done(((f32[128,128]{1,0:T(8,128)}), f32[4096,128]{1,0:T(8,128)}) %all-gather.6.cloned.1.call-update) | async-done | bytes 2097168 | tf_op jit(solution)/shard_map/all_gather | solution.py:54
  563.0 5.3 fusion.38
  578.5 5.1 collective-permute-start.13
  604.7 36.9 %psum.67 = f32[128]{0:T(128)S(1)} all-reduce(f32[128]{0:T(128)S(1)} %multiply_reduce_fusion.3), channel_id=1, replica_groups=mesh['sub'=32] {'sub'}, use_global_device_ids=true, to_apply=%region_25.27 | all-reduce | flops 128 | bytes 1024 | tf_op jit(solution)/shard_map/psum | solution.py:58
  643.8 4.9 fusion.29
  662.3 5.3 collective-permute-start.17
  690.4 37.0 %psum.68 = f32[128]{0:T(128)S(1)} all-reduce(f32[128]{0:T(128)S(1)} %multiply_reduce_fusion.2), channel_id=1, replica_groups=mesh['sub'=32] {'sub'}, use_global_device_ids=true, to_apply=%region_31.33 | all-reduce | flops 128 | bytes 1024 | tf_op jit(solution)/shard_map/psum | solution.py:70
  732.9 134.0 %all-reduce.9.cloned.1.call-done = f32[4096,128]{1,0:T(8,128)} async-done(((f32[4096,128]{1,0:T(8,128)}), f32[4096,128]{1,0:T(8,128)}) %all-reduce.9.cloned.1.call-update) | async-done | bytes 2097168 | tf_op jit(solution)/shard_map/psum | solution.py:52
  871.4 5.5 fusion.6
  876.9 49.9 %all-gather.8.cloned.1.call-done = f32[4096,128]{1,0:T(8,128)} async-done(((f32[128,128]{1,0:T(8,128)}), f32[4096,128]{1,0:T(8,128)}) %all-gather.8.cloned.1.call-update) | async-done | bytes 2097168 | tf_op jit(solution)/shard_map/all_gather | solution.py:54
  942.8 5.1 collective-permute-start.21
  969.9 37.2 %psum.70 = f32[128]{0:T(128)S(1)} all-reduce(f32[128]{0:T(128)S(1)} %multiply_reduce_fusion.1), channel_id=1, replica_groups=mesh['sub'=32] {'sub'}, use_global_device_ids=true, to_apply=%region_39.41 | all-reduce | flops 128 | bytes 1024 | tf_op jit(solution)/shard_map/psum | solution.py:58
  1007.1 5.4 fusion.32
  1023.1 5.3 collective-permute-start.25
  1050.8 37.0 %psum.71 = f32[128]{0:T(128)S(1)} all-reduce(f32[128]{0:T(128)S(1)} %multiply_reduce_fusion), channel_id=1, replica_groups=mesh['sub'=32] {'sub'}, use_global_device_ids=true, to_apply=%region_45.47 | all-reduce | flops 128 | bytes 1024 | tf_op jit(solution)/shard_map/psum | solution.py:70
  (218 shorter events, 270.8 us)
Async XLA Ops:
  7.2 161.0 %all-reduce.5.cloned.1.call-start = ((), (), s32[]{:S(2)}) async-start(), calls=%async_computation | async-start | bytes 4194304 | tf_op jit(solution)/shard_map/psum | solution.py:52
  10.9 14.8 %collective-permute-start = (f32[256,128]{1,0:T(8,128)}, f32[256,128]{1,0:T(8,128)S(1)}, u32[]{:S(2)}, u32[]{:S(2)}) collective-permute-start(f32[256,128]{1,0:T(8,128)} %broadcast_select_fusion.27), channel_id=1, source_target_pairs={{31,0},{0,1},{1,2},{2,3},{3,4},{4,5},{5,6},{6,7},{7,8},{8,9},{9,10... | collective-permute-start | bytes 393224 | tf_op jit(solution)/shard_map/ppermute | solution.py:17
  12.9 15.1 %collective-permute-start.1 = (f32[256,128]{1,0:T(8,128)}, f32[256,128]{1,0:T(8,128)S(1)}, u32[]{:S(2)}, u32[]{:S(2)}) collective-permute-start(f32[256,128]{1,0:T(8,128)} %broadcast_select_fusion.26), channel_id=1, source_target_pairs={{1,0},{2,1},{3,2},{4,3},{5,4},{6,5},{7,6},{8,7},{9,8},{10,9},{11,1... | collective-permute-start | bytes 393224 | tf_op jit(solution)/shard_map/ppermute | solution.py:17
  37.9 190.2 %all-gather.4.cloned.1.call-start = ((), (), s32[]{:S(2)}) async-start(), calls=%async_computation.1 | async-start | bytes 2162688 | tf_op jit(solution)/shard_map/all_gather | solution.py:54
  172.7 327.4 %all-reduce.7.cloned.1.call-start = ((), (), s32[]{:S(2)}) async-start(), calls=%async_computation.2 | async-start | bytes 4194304 | tf_op jit(solution)/shard_map/psum | solution.py:52
  250.3 14.6 %collective-permute-start.5 = (f32[256,128]{1,0:T(8,128)}, f32[256,128]{1,0:T(8,128)}, u32[]{:S(2)}, u32[]{:S(2)}) collective-permute-start(f32[256,128]{1,0:T(8,128)} %broadcast_select_fusion.22), channel_id=1, source_target_pairs={{1,0},{2,1},{3,2},{4,3},{5,4},{6,5},{7,6},{8,7},{9,8},{10,9},{11,1... | collective-permute-start | bytes 393224 | tf_op jit(solution)/shard_map/ppermute | solution.py:17
  256.1 12.9 %collective-permute-start.6 = (f32[256,128]{1,0:T(8,128)}, f32[256,128]{1,0:T(8,128)S(1)}, u32[]{:S(2)}, u32[]{:S(2)}) collective-permute-start(f32[256,128]{1,0:T(8,128)} %broadcast_select_fusion.21), channel_id=1, source_target_pairs={{24,0},{25,1},{26,2},{27,3},{28,4},{29,5},{30,6},{31,7},{0,8},{1,9... | collective-permute-start | bytes 393224 | tf_op jit(solution)/shard_map/ppermute | solution.py:17
  256.9 15.9 %collective-permute-start.7 = (f32[256,128]{1,0:T(8,128)}, f32[256,128]{1,0:T(8,128)S(1)}, u32[]{:S(2)}, u32[]{:S(2)}) collective-permute-start(f32[256,128]{1,0:T(8,128)} %broadcast_select_fusion.20), channel_id=1, source_target_pairs={{8,0},{9,1},{10,2},{11,3},{12,4},{13,5},{14,6},{15,7},{16,8},{17,9... | collective-permute-start | bytes 393224 | tf_op jit(solution)/shard_map/ppermute | solution.py:17
  293.6 12.4 %collective-permute-start.8 = (f32[256,128]{1,0:T(8,128)S(1)}, f32[256,128]{1,0:T(8,128)}, u32[]{:S(2)}, u32[]{:S(2)}) collective-permute-start(f32[256,128]{1,0:T(8,128)S(1)} %broadcast_select_fusion.19), channel_id=1, source_target_pairs={{31,0},{0,1},{1,2},{2,3},{3,4},{4,5},{5,6},{6,7},{7,8},{8,9},{9,10... | collective-permute-start | bytes 393224 | tf_op jit(solution)/shard_map/ppermute | solution.py:17
  295.3 14.8 %collective-permute-start.9 = (f32[256,128]{1,0:T(8,128)}, f32[256,128]{1,0:T(8,128)}, u32[]{:S(2)}, u32[]{:S(2)}) collective-permute-start(f32[256,128]{1,0:T(8,128)} %broadcast_select_fusion.18), channel_id=1, source_target_pairs={{1,0},{2,1},{3,2},{4,3},{5,4},{6,5},{7,6},{8,7},{9,8},{10,9},{11,1... | collective-permute-start | bytes 393224 | tf_op jit(solution)/shard_map/ppermute | solution.py:17
  301.4 12.8 %collective-permute-start.10 = (f32[256,128]{1,0:T(8,128)}, f32[256,128]{1,0:T(8,128)S(1)}, u32[]{:S(2)}, u32[]{:S(2)}) collective-permute-start(f32[256,128]{1,0:T(8,128)} %broadcast_select_fusion.17), channel_id=1, source_target_pairs={{24,0},{25,1},{26,2},{27,3},{28,4},{29,5},{30,6},{31,7},{0,8},{1,9... | collective-permute-start | bytes 393224 | tf_op jit(solution)/shard_map/ppermute | solution.py:17
  302.2 16.2 %collective-permute-start.11 = (f32[256,128]{1,0:T(8,128)}, f32[256,128]{1,0:T(8,128)S(1)}, u32[]{:S(2)}, u32[]{:S(2)}) collective-permute-start(f32[256,128]{1,0:T(8,128)} %broadcast_select_fusion.16), channel_id=1, source_target_pairs={{8,0},{9,1},{10,2},{11,3},{12,4},{13,5},{14,6},{15,7},{16,8},{17,9... | collective-permute-start | bytes 393224 | tf_op jit(solution)/shard_map/ppermute | solution.py:17
  365.7 194.3 %all-gather.6.cloned.1.call-start = ((), (), s32[]{:S(2)}) async-start(), calls=%async_computation.3 | async-start | bytes 2162688 | tf_op jit(solution)/shard_map/all_gather | solution.py:54
  504.6 362.4 %all-reduce.9.cloned.1.call-start = ((), (), s32[]{:S(2)}) async-start(), calls=%async_computation.4 | async-start | bytes 4194304 | tf_op jit(solution)/shard_map/psum | solution.py:52
  578.5 13.0 %collective-permute-start.13 = (f32[256,128]{1,0:T(8,128)S(1)}, f32[256,128]{1,0:T(8,128)S(1)}, u32[]{:S(2)}, u32[]{:S(2)}) collective-permute-start(f32[256,128]{1,0:T(8,128)S(1)} %broadcast_select_fusion.14), channel_id=1, source_target_pairs={{1,0},{2,1},{3,2},{4,3},{5,4},{6,5},{7,6},{8,7},{9,8},{10,9},{11,1... | collective-permute-start | bytes 393224 | tf_op jit(solution)/shard_map/ppermute | solution.py:17
  583.9 15.3 %collective-permute-start.15 = (f32[256,128]{1,0:T(8,128)S(1)}, f32[256,128]{1,0:T(8,128)S(1)}, u32[]{:S(2)}, u32[]{:S(2)}) collective-permute-start(f32[256,128]{1,0:T(8,128)S(1)} %broadcast_select_fusion.12), channel_id=1, source_target_pairs={{8,0},{9,1},{10,2},{11,3},{12,4},{13,5},{14,6},{15,7},{16,8},{17,9... | collective-permute-start | bytes 393224 | tf_op jit(solution)/shard_map/ppermute | solution.py:17
  662.3 14.8 %collective-permute-start.17 = (f32[256,128]{1,0:T(8,128)}, f32[256,128]{1,0:T(8,128)}, u32[]{:S(2)}, u32[]{:S(2)}) collective-permute-start(f32[256,128]{1,0:T(8,128)} %broadcast_select_fusion.10), channel_id=1, source_target_pairs={{1,0},{2,1},{3,2},{4,3},{5,4},{6,5},{7,6},{8,7},{9,8},{10,9},{11,1... | collective-permute-start | bytes 393224 | tf_op jit(solution)/shard_map/ppermute | solution.py:17
  668.4 12.8 %collective-permute-start.18 = (f32[256,128]{1,0:T(8,128)}, f32[256,128]{1,0:T(8,128)S(1)}, u32[]{:S(2)}, u32[]{:S(2)}) collective-permute-start(f32[256,128]{1,0:T(8,128)} %broadcast_select_fusion.9), channel_id=1, source_target_pairs={{24,0},{25,1},{26,2},{27,3},{28,4},{29,5},{30,6},{31,7},{0,8},{1,9... | collective-permute-start | bytes 393224 | tf_op jit(solution)/shard_map/ppermute | solution.py:17
  670.2 14.8 %collective-permute-start.19 = (f32[256,128]{1,0:T(8,128)}, f32[256,128]{1,0:T(8,128)S(1)}, u32[]{:S(2)}, u32[]{:S(2)}) collective-permute-start(f32[256,128]{1,0:T(8,128)} %broadcast_select_fusion.8), channel_id=1, source_target_pairs={{8,0},{9,1},{10,2},{11,3},{12,4},{13,5},{14,6},{15,7},{16,8},{17,9... | collective-permute-start | bytes 393224 | tf_op jit(solution)/shard_map/ppermute | solution.py:17
  732.6 194.2 %all-gather.8.cloned.1.call-start = ((), (), s32[]{:S(2)}) async-start(), calls=%async_computation.5 | async-start | bytes 2162688 | tf_op jit(solution)/shard_map/all_gather | solution.py:54
  942.8 14.2 %collective-permute-start.21 = (f32[256,128]{1,0:T(8,128)}, f32[256,128]{1,0:T(8,128)S(1)}, u32[]{:S(2)}, u32[]{:S(2)}) collective-permute-start(f32[256,128]{1,0:T(8,128)} %broadcast_select_fusion.6), channel_id=1, source_target_pairs={{1,0},{2,1},{3,2},{4,3},{5,4},{6,5},{7,6},{8,7},{9,8},{10,9},{11,1... | collective-permute-start | bytes 393224 | tf_op jit(solution)/shard_map/ppermute | solution.py:17
  949.4 15.1 %collective-permute-start.23 = (f32[256,128]{1,0:T(8,128)}, f32[256,128]{1,0:T(8,128)S(1)}, u32[]{:S(2)}, u32[]{:S(2)}) collective-permute-start(f32[256,128]{1,0:T(8,128)} %broadcast_select_fusion.4), channel_id=1, source_target_pairs={{8,0},{9,1},{10,2},{11,3},{12,4},{13,5},{14,6},{15,7},{16,8},{17,9... | collective-permute-start | bytes 393224 | tf_op jit(solution)/shard_map/ppermute | solution.py:17
  1023.1 14.4 %collective-permute-start.25 = (f32[256,128]{1,0:T(8,128)}, f32[256,128]{1,0:T(8,128)S(1)}, u32[]{:S(2)}, u32[]{:S(2)}) collective-permute-start(f32[256,128]{1,0:T(8,128)} %broadcast_select_fusion.2), channel_id=1, source_target_pairs={{1,0},{2,1},{3,2},{4,3},{5,4},{6,5},{7,6},{8,7},{9,8},{10,9},{11,1... | collective-permute-start | bytes 393224 | tf_op jit(solution)/shard_map/ppermute | solution.py:17
  1031.0 14.2 %collective-permute-start.27 = (f32[256,128]{1,0:T(8,128)}, f32[256,128]{1,0:T(8,128)S(1)}, u32[]{:S(2)}, u32[]{:S(2)}) collective-permute-start(f32[256,128]{1,0:T(8,128)} %broadcast_select_fusion), channel_id=1, source_target_pairs={{8,0},{9,1},{10,2},{11,3},{12,4},{13,5},{14,6},{15,7},{16,8},{17,9... | collective-permute-start | bytes 393224 | tf_op jit(solution)/shard_map/ppermute | solution.py:17
  (20 other events, 564.9 us)
Sparse Core Ops, SparseCore 0:
  38.1 130.0 all-reduce.4
  172.8 55.2 all-gather.3
  365.8 134.1 all-reduce.6
  504.7 55.2 all-gather.5
  732.8 134.1 all-reduce.8
  871.6 55.2 all-gather.7
where the time goes:
time: 1110 us; the launch traced here: 1100 us
  waiting for transfers between devices  559 us (50%)
  blocking collectives  185 us (17%)
  other arithmetic  145 us (13%)
  local copies, waits for them, and re-layouts  76.1 us (7%)
  starting transfers between devices  66.3 us (6%)
  matrix products  51.4 us (5%)
  between operations  15 us (1%)
    psum x3, waiting for transfers between devices, precond(): full_total = lax.psum(placed, 'sub')  399 us
    all_gather x3, waiting for transfers between devices, precond(): coarse_values = lax.all_gather(owned_values, 'sub', axis=0, tiled=True)  160 us
    psum x3, blocking collectives, precond(): lax.psum(jnp.sum(weights[:, None] * resid * result, axis=0), 'sub')  111 us
    scatter-add x28, other arithmetic, assemble(): assembled.at[row_lists[opposite_slot[slot_index]]].add(arrived, mode='drop')  103 us
    psum x2, blocking collectives, body(): lax.psum(jnp.sum(weights[:, None] * direction * image, axis=0), 'sub')  74 us
    ppermute x28, starting transfers between devices, shifted(): return lax.ppermute(block, axis, route)  65.6 us
    gather x28, local copies, waits for them, and re-layouts, assemble(): jnp.take(local, row_lists[slot_index], axis=0, mode='fill', fill_value=0.0)  51.1 us
  transfers between devices with their start and end apart: 34, of which 6 were waited for; matrix products, arithmetic and copies ran while one was open for 9% of the time, Pallas kernels for 0%

commit v1 on v0

v1 whole, which is shorter than its diff:
```python
import jax
import jax.numpy as jnp
from jax import lax
from jax.experimental import pallas as pl
from jax.experimental.pallas import tpu as pltpu
from jax.sharding import PartitionSpec as P

STRIDE = 8
F32 = jnp.float32
BF16 = jnp.bfloat16
TILE = 512
SCAL = 8
LANES = 128

VSPEC = pl.BlockSpec(memory_space=pltpu.VMEM)
SSPEC = pl.BlockSpec(memory_space=pltpu.SMEM)


def near(shape, dtype=F32):
    return jax.ShapeDtypeStruct(shape, dtype)


def far(shape, dtype=F32):
    return jax.ShapeDtypeStruct(shape, dtype)


def call(kernel, name, args, outs, scratch=(), specs=None, flops=0):
    specs = specs or {}
    return pl.pallas_call(
        kernel,
        name=name,
        out_shape=tuple(outs),
        in_specs=[specs.get(i, VSPEC) for i in range(len(args))],
        out_specs=tuple(VSPEC for _ in outs),
        scratch_shapes=list(scratch),
        compiler_params=pltpu.CompilerParams(vmem_limit_bytes=48 * 1024 * 1024),
        cost_estimate=pl.CostEstimate(
            flops=flops, bytes_accessed=8 * 1024 * 1024, transcendentals=0
        ),
    )(*args)


def cut(x):
    high = x.astype(BF16)
    return high, (x - high.astype(F32)).astype(BF16)


def pair(x):
    return jnp.concatenate(cut(x), axis=1)


def halves(product):
    half = product.shape[1] // 2
    return product[:, :half] + product[:, half:]


def three(product, rows):
    half = product.shape[1] // 2
    return product[:rows, :half] + product[:rows, half:] + product[rows : 2 * rows, :half]


def dot(a, b):
    return jnp.dot(a, b, preferred_element_type=F32)


def tiles(total):
    step = min(TILE, total)
    return [(lo, min(step, total - lo)) for lo in range(0, total, step)]


def folded(x):
    return jnp.sum(x.reshape(-1, 8, x.shape[-1]), axis=0)


def pick_out(pick_ref, cat_ref, out_refs):
    cap = out_refs[0].shape[0]
    for j, out in enumerate(out_refs):
        out[...] = halves(dot(pick_ref[j * cap : (j + 1) * cap, :], cat_ref[...]))


def arrivals(arrived_refs, arr_cat):
    cap = arrived_refs[0].shape[0]
    for j, ref in enumerate(arrived_refs):
        arr_cat[j * cap : (j + 1) * cap, :] = pair(ref[...])


def setup_kernel(row_ref, col_ref, count_ref, basis_ref, basis_t_ref, loads_ref,
                 pick_ref, place_ref, weight_ref, basis2_ref, basis3_ref,
                 out0, out1, out2, out3, cat):
    slots, rows = pick_ref.shape
    rhs = loads_ref.shape[1]
    for lo, n in tiles(slots):
        at = lax.broadcasted_iota(jnp.int32, (n, rows), 1)
        pick_ref[lo : lo + n, :] = jnp.where(at == col_ref[lo : lo + n, :], 1.0, 0.0).astype(BF16)
    for lo, n in tiles(rows):
        cat[lo : lo + n, :] = pair(loads_ref[lo : lo + n, :])
    pick_out(pick_ref, cat, (out0, out1, out2, out3))
    for lo, n in tiles(rows):
        at = lo + lax.broadcasted_iota(jnp.int32, (n, slots), 0)
        place_ref[lo : lo + n, :] = jnp.where(at == row_ref[...], 1.0, 0.0).astype(BF16)
        weight = 1.0 / count_ref[lo : lo + n, :].astype(F32)
        weight_ref[lo : lo + n, :] = jnp.broadcast_to(weight, (n, rhs))
    ncl = basis_ref.shape[0]
    high, low = cut(basis_ref[...])
    basis2_ref[:ncl, :] = high
    basis2_ref[ncl:, :] = low
    high, low = cut(basis_t_ref[...])
    basis3_ref[...] = jnp.concatenate([high, high, low], axis=1)


def columns_kernel(map_ref, inverse_ref, out_ref, turned):
    order = inverse_ref.shape[1]
    for lo, n in tiles(order):
        turned[lo : lo + n, :] = inverse_ref[:, lo : lo + n].T

    def step(i, _):
        for k in range(8):
            m = i * 8 + k
            out_ref[pl.ds(m, 1), :] = turned[pl.ds(map_ref[m], 1), :]
        return 0

    lax.fori_loop(0, out_ref.shape[0] // 8, step, 0)


def coarse_kernel(map_ref, which_ref, got_ref, keep_ref, send_ref, turned, rowed):
    ncl, half = keep_ref.shape
    width = got_ref.shape[1]
    fill = jnp.zeros((turned.shape[1] - ncl, width), F32)
    for t in range(got_ref.shape[0] // ncl):
        block = jnp.concatenate([got_ref[t * ncl : (t + 1) * ncl, :], fill], axis=0)
        turned[t * width : (t + 1) * width, :] = block.T

    def step(i, _):
        for k in range(8):
            m = i * 8 + k
            rowed[pl.ds(m, 1), :] = turned[pl.ds(map_ref[m], 1), :]
        return 0

    lax.fori_loop(0, rowed.shape[0] // 8, step, 0)
    first = rowed[:half, :].T[:ncl, :]
    second = rowed[half:, :].T[:ncl, :]
    even = which_ref[0] == 0
    keep_ref[...] = jnp.where(even, first, second)
    send_ref[...] = jnp.where(even, second, first)


def stack_kernel(own_ref, other_ref, out_ref):
    ncl = own_ref.shape[0]
    own_high, own_low = cut(own_ref[...])
    other_high, other_low = cut(other_ref[...])
    out_ref[:ncl, :] = own_high
    out_ref[ncl : 2 * ncl, :] = other_high
    out_ref[2 * ncl : 3 * ncl, :] = own_low
    out_ref[3 * ncl :, :] = other_low


def send_terms(terms, scalars, send_ref):
    block = jnp.concatenate([terms, scalars], axis=0)
    rows = block.shape[0]
    for g in range(send_ref.shape[0] // rows):
        send_ref[g * rows : (g + 1) * rows, :] = block


def front(inverse_ref, cat, local_ref):
    for lo, n in tiles(inverse_ref.shape[0]):
        local_ref[lo : lo + n, :] = halves(dot(inverse_ref[lo : lo + n, :], cat[...]))


def first_kernel(loads_ref, a0, a1, a2, a3, place_ref, weight_ref, basis2_ref, inverse_ref,
                 resid_ref, local_ref, send_ref, cat, arr_cat):
    ncl = basis2_ref.shape[0] // 2
    rhs = loads_ref.shape[1]
    arrivals((a0, a1, a2, a3), arr_cat)
    terms = jnp.zeros((2 * ncl, 2 * rhs), F32)
    for lo, n in tiles(loads_ref.shape[0]):
        at = slice(lo, lo + n)
        resid = loads_ref[at, :] + halves(dot(place_ref[at, :], arr_cat[...]))
        resid_ref[at, :] = resid
        both = pair(weight_ref[at, :] * resid)
        cat[at, :] = both
        terms += dot(basis2_ref[:, at], both)
    send_terms(three(terms, ncl), jnp.zeros((SCAL, rhs), F32), send_ref)
    front(inverse_ref, cat, local_ref)


def coarse_solve_kernel(got_ref, g_ref, own_ref, other_ref):
    ncl = g_ref.shape[0] // 4
    rows = ncl + SCAL
    groups = got_ref.shape[0] // rows
    got = got_ref[...].reshape(groups, rows, got_ref.shape[1])
    terms = got[:, :ncl].reshape(groups * ncl, got_ref.shape[1])
    scalars = jnp.sum(got[:, ncl:], axis=0)
    values = three(dot(g_ref[...], pair(terms)), 2 * ncl)
    own_ref[:ncl, :] = values[:ncl]
    own_ref[ncl:, :] = scalars
    other_ref[:ncl, :] = values[ncl:]
    other_ref[ncl:, :] = scalars


def back_kernel(own_ref, other_ref, local_ref, weight_ref, basis3_ref, pick_ref,
                field_ref, scal_ref, out0, out1, out2, out3, cat):
    ncl = own_ref.shape[0] - SCAL
    total = own_ref[...] + other_ref[...]
    scal_ref[...] = total[ncl:]
    high, low = cut(total[:ncl])
    values = jnp.concatenate([high, low, high], axis=0)
    for lo, n in tiles(local_ref.shape[0]):
        at = slice(lo, lo + n)
        field = weight_ref[at, :] * (local_ref[at, :] + dot(basis3_ref[at, :], values))
        field_ref[at, :] = field
        cat[at, :] = pair(field)
    pick_out(pick_ref, cat, (out0, out1, out2, out3))


def apply_kernel(part_ref, a0, a1, a2, a3, place_ref, stiff_ref, pick_ref,
                 field_ref, image_ref, out0, out1, out2, out3, cat, arr_cat, cat2):
    arrivals((a0, a1, a2, a3), arr_cat)
    for lo, n in tiles(part_ref.shape[0]):
        at = slice(lo, lo + n)
        field = part_ref[at, :] + halves(dot(place_ref[at, :], arr_cat[...]))
        field_ref[at, :] = field
        cat[at, :] = pair(field)
    for lo, n in tiles(part_ref.shape[0]):
        at = slice(lo, lo + n)
        image = halves(dot(stiff_ref[at, :], cat[...]))
        image_ref[at, :] = image
        cat2[at, :] = pair(image)
    pick_out(pick_ref, cat2, (out0, out1, out2, out3))


def collect(sums, rhs):
    rows = [jnp.sum(s, axis=0, keepdims=True) for s in sums]
    rows.append(jnp.zeros((SCAL - len(rows), rhs), F32))
    return jnp.concatenate(rows, axis=0)


def start_kernel(part_ref, a0, a1, a2, a3, r_ref, u_ref,
                 place_ref, weight_ref, basis2_ref, inverse_ref,
                 w_ref, local_ref, send_ref, cat, arr_cat):
    ncl = basis2_ref.shape[0] // 2
    rhs = r_ref.shape[1]
    arrivals((a0, a1, a2, a3), arr_cat)
    terms = jnp.zeros((2 * ncl, 2 * rhs), F32)
    ru = jnp.zeros((8, rhs), F32)
    uw = jnp.zeros((8, rhs), F32)
    for lo, n in tiles(r_ref.shape[0]):
        at = slice(lo, lo + n)
        w = part_ref[at, :] + halves(dot(place_ref[at, :], arr_cat[...]))
        w_ref[at, :] = w
        weight = weight_ref[at, :]
        scaled = weight * w
        weighted = weight * u_ref[at, :]
        ru += folded(weighted * r_ref[at, :])
        uw += folded(weighted * w)
        both = pair(scaled)
        cat[at, :] = both
        terms += dot(basis2_ref[:, at], both)
    send_terms(three(terms, ncl), collect([ru, uw], rhs), send_ref)
    front(inverse_ref, cat, local_ref)


def second_kernel(part_ref, a0, a1, a2, a3, scal_ref, r_ref, u_ref, w_ref, m_ref,
                  place_ref, weight_ref, basis2_ref, inverse_ref,
                  z_ref, x1_ref, r1_ref, u1_ref, w1_ref, local_ref, send_ref,
                  cat, arr_cat):
    ncl = basis2_ref.shape[0] // 2
    rhs = r_ref.shape[1]
    arrivals((a0, a1, a2, a3), arr_cat)
    alpha = scal_ref[0:1, :] / scal_ref[1:2, :]
    terms = jnp.zeros((2 * ncl, 2 * rhs), F32)
    sums = [jnp.zeros((8, rhs), F32) for _ in range(4)]
    for lo, n in tiles(r_ref.shape[0]):
        at = slice(lo, lo + n)
        z = part_ref[at, :] + halves(dot(place_ref[at, :], arr_cat[...]))
        z_ref[at, :] = z
        weight = weight_ref[at, :]
        p, s = u_ref[at, :], w_ref[at, :]
        x1_ref[at, :] = alpha * p
        r1 = r_ref[at, :] - alpha * s
        u1 = p - alpha * m_ref[at, :]
        w1 = s - alpha * z
        r1_ref[at, :] = r1
        u1_ref[at, :] = u1
        w1_ref[at, :] = w1
        weighted = weight * u1
        scaled = weight * w1
        for k, term in enumerate((weighted * r1, weighted * w1, weighted * s, scaled * p)):
            sums[k] += folded(term)
        both = pair(scaled)
        cat[at, :] = both
        terms += dot(basis2_ref[:, at], both)
    send_terms(three(terms, ncl), collect(sums, rhs), send_ref)
    front(inverse_ref, cat, local_ref)


def step_scalars(before, now):
    beta = now[0:1, :] / before[0:1, :]
    energy = now[1:2, :] + beta * (now[2:3, :] + now[3:4, :]) + beta * beta * before[1:2, :]
    return beta, now[0:1, :] / energy, energy


def third_kernel(before_ref, scal_ref, x1_ref, r1_ref, u1_ref, w1_ref, p_ref, s_ref, q_ref, z_ref,
                 m_ref, image_ref, weight_ref,
                 x2_ref, r2_ref, u2_ref, half_ref, p1_ref, s1_ref, state_ref, send_ref):
    rhs = r1_ref.shape[1]
    beta, alpha, energy = step_scalars(before_ref[...], scal_ref[...])
    sums = [jnp.zeros((8, rhs), F32) for _ in range(4)]
    for lo, n in tiles(r1_ref.shape[0]):
        at = slice(lo, lo + n)
        p1 = u1_ref[at, :] + beta * p_ref[at, :]
        s1 = w1_ref[at, :] + beta * s_ref[at, :]
        q1 = m_ref[at, :] + beta * q_ref[at, :]
        r2 = r1_ref[at, :] - alpha * s1
        u2 = u1_ref[at, :] - alpha * q1
        half = w1_ref[at, :] - (alpha * beta) * z_ref[at, :]
        x2_ref[at, :] = x1_ref[at, :] + alpha * p1
        r2_ref[at, :] = r2
        u2_ref[at, :] = u2
        half_ref[at, :] = half
        p1_ref[at, :] = p1
        s1_ref[at, :] = s1
        weight = weight_ref[at, :]
        left = weight * half - alpha * image_ref[at, :]
        weighted = weight * u2
        for k, term in enumerate((weighted * r2, u2 * left, weighted * s1, p1 * left)):
            sums[k] += folded(term)
    block = collect(sums, rhs)
    for g in range(send_ref.shape[0] // SCAL):
        send_ref[g * SCAL : (g + 1) * SCAL, :] = block
    state_ref[...] = jnp.concatenate(
        [scal_ref[0:1, :], energy, alpha, jnp.zeros((SCAL - 3, rhs), F32)], axis=0
    )


def last_kernel(state_ref, got_ref, image_ref, a0, a1, a2, a3, place_ref,
                x2_ref, r2_ref, u2_ref, half_ref, p1_ref, s1_ref,
                x3_ref, r3_ref, arr_cat):
    arrivals((a0, a1, a2, a3), arr_cat)
    state = state_ref[...]
    now = jnp.sum(got_ref[...].reshape(-1, SCAL, got_ref.shape[1]), axis=0)
    beta, alpha, _ = step_scalars(state, now)
    old = state[2:3, :]
    for lo, n in tiles(r2_ref.shape[0]):
        at = slice(lo, lo + n)
        image = image_ref[at, :] + halves(dot(place_ref[at, :], arr_cat[...]))
        w2 = half_ref[at, :] - old * image
        x3_ref[at, :] = x2_ref[at, :] + alpha * (u2_ref[at, :] + beta * p1_ref[at, :])
        r3_ref[at, :] = r2_ref[at, :] - alpha * (w2 + beta * s1_ref[at, :])


def body(
    stiffness, local_inverse, coarse_basis, loads, counts, shared_rows, coarse_map, coarse_inverse
):
    size = lax.axis_size("sub")
    me = lax.axis_index("sub")
    rows, rhs = loads.shape[1:]
    ncl = coarse_basis.shape[1]
    slots, cap = shared_rows.shape[1:]
    order = coarse_inverse.shape[1]
    lists = slots * cap
    stiff, inverse = stiffness[0], local_inverse[0]

    def partner(distance, parity):
        def of(i):
            up = (i // distance) % 2 == parity
            return (i + distance if up else i - distance) % size

        return [(i, of(i)) for i in range(size)]

    swaps = [partner(1, 0), partner(1, 1), partner(STRIDE, 0), partner(STRIDE, 1)]

    def exchange(outs):
        got = [None] * len(outs)
        for j in (3, 2, 1, 0):
            got[j] = lax.ppermute(outs[j], "sub", swaps[j])
        return got

    cores = [[2 * i + c for i in range(size // 2)] for c in range(2)]
    groups = size // 2
    block = ncl + SCAL

    up_one = me % 2 == 0
    up_far = (me // STRIDE) % 2 == 0
    given = shared_rows[0]
    mine = jnp.concatenate(
        [
            jnp.where(up_one, given[:2], given[1::-1]),
            jnp.where(up_far, given[2:], given[:1:-1]),
        ],
        axis=0,
    )

    maps = lax.all_gather(coarse_map[0], "sub", axis=0, tiled=True)

    fields = (rows, rhs)
    out4 = [far((cap, rhs))] * 4
    wide = pltpu.VMEM((rows, 2 * rhs), BF16)
    wide_arr = pltpu.VMEM((lists, 2 * rhs), BF16)

    pick, place, weight, basis2, basis3, *outs = call(
        setup_kernel,
        "lists_and_loads",
        (
            mine.reshape(1, lists),
            mine.reshape(lists, 1),
            counts[0].reshape(rows, 1),
            coarse_basis[0],
            coarse_basis[0].T,
            loads[0],
        ),
        [
            near((lists, rows), BF16),
            near((rows, lists), BF16),
            near(fields),
            near((2 * ncl, rows), BF16),
            near((rows, 3 * ncl), BF16),
        ]
        + out4,
        [wide],
    )
    got = exchange(outs)
    r0, local, send = call(
        first_kernel,
        "residual_and_terms",
        (loads[0], *got, place, weight, basis2, inverse),
        [near(fields), near(fields), far((groups * block, rhs))],
        [wide, wide_arr],
    )

    (picked,) = call(
        columns_kernel,
        "coarse_columns",
        (maps, coarse_inverse),
        [far((size * ncl, coarse_inverse.shape[0]))],
        [pltpu.VMEM((order, coarse_inverse.shape[0]), F32)],
        {0: SSPEC},
    )
    mine_rows = lax.all_to_all(picked, "sub", 0, 0, tiled=True)
    by_core = maps.reshape(groups, 2, ncl).swapaxes(0, 1).reshape(-1)
    keep, pass_on = call(
        coarse_kernel,
        "coarse_block",
        (by_core, (me % 2).reshape(1), mine_rows),
        [far((ncl, groups * ncl)), far((ncl, groups * ncl))],
        [
            pltpu.VMEM((order, LANES), F32),
            pltpu.VMEM((size * ncl, LANES), F32),
        ],
        {0: SSPEC, 1: SSPEC},
    )
    passed = lax.ppermute(pass_on, "sub", swaps[0])
    (coarse,) = call(
        stack_kernel, "coarse_addends", (keep, passed), [near((4 * ncl, groups * ncl), BF16)]
    )

    def middle(send, local):
        got = lax.all_to_all(send, "sub", 0, 0, tiled=True, axis_index_groups=cores)
        own, other = call(
            coarse_solve_kernel,
            "coarse_solve",
            (got, coarse),
            [far((block, rhs)), far((block, rhs))],
        )
        came = lax.ppermute(other, "sub", swaps[0])
        part, scal, *outs = call(
            back_kernel,
            "coarse_back",
            (own, came, local, weight, basis3, pick),
            [near(fields), near((SCAL, rhs))] + out4,
            [wide],
        )
        arrived = exchange(outs)
        field, image, *outs = call(
            apply_kernel,
            "operator",
            (part, *arrived, place, stiff, pick),
            [near(fields), near(fields)] + out4,
            [wide, wide_arr, wide],
        )
        return scal, field, image, outs

    _, u0, image, outs = middle(send, local)
    got = exchange(outs)
    w0, local, send = call(
        start_kernel,
        "start",
        (image, *got, r0, u0, place, weight, basis2, inverse),
        [near(fields), near(fields), far((groups * block, rhs))],
        [wide, wide_arr],
    )
    scal0, m0, image, outs = middle(send, local)
    got = exchange(outs)
    z0, x1, r1, u1, w1, local, send = call(
        second_kernel,
        "first_update",
        (image, *got, scal0, r0, u0, w0, m0, place, weight, basis2, inverse),
        [near(fields)] * 6 + [far((groups * block, rhs))],
        [wide, wide_arr],
    )
    scal1, m1, image, outs = middle(send, local)
    got = exchange(outs)
    x2, r2, u2, half, p1, s1, state, send = call(
        third_kernel,
        "second_update",
        (scal0, scal1, x1, r1, u1, w1, u0, w0, m0, z0, m1, image, weight),
        [near(fields)] * 6 + [near((SCAL, rhs)), far((size * SCAL, rhs))],
    )
    sums = lax.all_to_all(send, "sub", 0, 0, tiled=True)
    x3, r3 = call(
        last_kernel,
        "last_update",
        (state, sums, image, *got, place, x2, r2, u2, half, p1, s1),
        [far(fields), far(fields)],
        [wide_arr],
    )
    return (x3[None], r3[None])


def solution(mesh):
    placed = (
        P("sub", None, None),
        P("sub", None, None),
        P("sub", None, None),
        P("sub", None, None),
        P("sub", None),
        P("sub", None, None),
        P("sub", None),
        P("sub", None),
    )
    return jax.shard_map(
        body,
        mesh=mesh,
        in_specs=placed,
        out_specs=(P("sub", None, None), P("sub", None, None)),
        check_vma=False,
    )
```

time: 1110 us -> 298 us (0.27)
  waiting for transfers between devices: 559 us -> 58.3 us
  other arithmetic: 145 us -> 0.02 us
  blocking collectives: 185 us -> 78.8 us
  Pallas kernels: 0 us -> 76.7 us
  matrix products: 51.4 us -> 0 us
  local copies, waits for them, and re-layouts: 76.1 us -> 27.1 us
  between operations: 15 us -> 1.07 us
  starting transfers between devices: 66.3 us -> 55 us
    psum x3 -> x0, waiting for transfers between devices: 399 us -> none  [precond(): full_total = lax.psum(placed, 'sub')]
    psum x5 -> x0, blocking collectives: 185 us -> none  [the longest x3 111 us: precond(): lax.psum(jnp.sum(weights[:, None] * resid * result, axis=0), 'sub')]
    all_gather x3 -> x0, waiting for transfers between devices: 160 us -> none  [precond(): coarse_values = lax.all_gather(owned_values, 'sub', axis=0, tiled=True)]
    scatter-add x31 -> x0, other arithmetic: 109 us -> none  [the longest x28 103 us: assemble(): assembled.at[row_lists[opposite_slot[slot_index]]].add(arrived, mode='drop')]
    pallas_call x0 -> x18, Pallas kernels: none -> 76.7 us  [call(): pl.pallas_call(kernel, name=name, out_shape=tuple(outs), in_specs=[specs....]
    gather x31 -> x0, local copies, waits for them, and re-layouts: 57.6 us -> none  [the longest x28 51.1 us: assemble(): jnp.take(local, row_lists[slot_index], axis=0, mode='fill', fill_value=0.0)]
    dot_general x15 -> x0, matrix products: 51.4 us -> none  [the longest x3 16 us: precond(): jnp.dot(inverse_block, scaled.astype(jnp.bfloat16), preferred_element_typ...]
    ppermute x28 -> x32, waiting for transfers between devices: 0.07 us -> 50.3 us  [the longest x28 45.4 us: exchange(): got[j] = lax.ppermute(outs[j], 'sub', swaps[j])]
  transfers between devices with their start and end apart: 34 -> 35, of which waited for: 6 -> 23; matrix products, arithmetic and copies ran while one was open for 9% -> 1% of each run, Pallas kernels for 0% -> 5%
where the time goes in v1:
time: 298 us; the launch traced here: 297 us
  blocking collectives  78.8 us (26%)
  Pallas kernels  76.7 us (26%)
  waiting for transfers between devices  58.3 us (20%)
  starting transfers between devices  55 us (18%)
  local copies, waits for them, and re-layouts  27.1 us (9%)
    pallas_call x18, Pallas kernels, call(): pl.pallas_call(kernel, name=name, out_shape=tuple(outs), in_specs=[specs....  76.7 us
    ppermute x28, waiting for transfers between devices, exchange(): got[j] = lax.ppermute(outs[j], 'sub', swaps[j])  45.4 us
    all_gather x1, blocking collectives, body(): maps = lax.all_gather(coarse_map[0], 'sub', axis=0, tiled=True)  42 us
    ppermute x28, starting transfers between devices, exchange(): got[j] = lax.ppermute(outs[j], 'sub', swaps[j])  39.6 us
    all_to_all x2, blocking collectives, middle(): got = lax.all_to_all(send, 'sub', 0, 0, tiled=True, axis_index_groups=cores)  36.8 us
    unnamed x83, local copies, waits for them, and re-layouts  26.5 us
    all_to_all x1, waiting for transfers between devices, middle(): got = lax.all_to_all(send, 'sub', 0, 0, tiled=True, axis_index_groups=cores)  8.06 us
    all_to_all x1, starting transfers between devices, middle(): got = lax.all_to_all(send, 'sub', 0, 0, tiled=True, axis_index_groups=cores)  6.96 us
  transfers between devices with their start and end apart: 35, of which 23 were waited for; matrix products, arithmetic and copies ran while one was open for 1% of the time, Pallas kernels for 5%

profile of v1, /device:TPU:0, one launch (start us, length us, event | category | flops | bytes accessed | tf_op | source)
XLA Modules:
  0.0 297.0 jit_solution(6043738281240712870)
XLA Ops:
  1.4 42.0 %all-reduce.map_ref = s32[1536]{0:T(1024)S(1)} all-reduce(s32[1536]{0:T(1024)S(1)} %bitcast_dynamic-update-slice_fusion), channel_id=2, replica_groups=mesh['sub'=32] {'sub'}, use_global_device_ids=true, to_apply=%add | all-reduce | flops 1536 | bytes 12288 | tf_op jit(solution)/shard_map/all_gather | solution.py:393
  45.1 4.2 %coarse_columns.1 = f32[1536,128]{1,0:T(8,128)} custom-call(s32[1536]{0:T(1024)S(1)} %all-reduce.map_ref, f32[128,4096]{1,0:T(8,128)S(1)} %copy-done.13), custom_call_target="tpu_custom_call" | custom-call | bytes 8388608 | tf_op jit(solution)/shard_map/coarse_columns/pallas_call | solution.py:29
  49.3 4.5 %all-to-all-start.1 = ((f32[32,48,128]{2,1,0:T(8,128)}), f32[32,48,128]{2,1,0:T(8,128)}, u32[]{:S(2)}, u32[]{:S(2)}) async-start(f32[32,48,128]{2,1,0:T(8,128)} %bitcast.13), calls=%async_computation.1 | async-start | bytes 1572864 | tf_op jit(solution)/shard_map/all_to_all | solution.py:438
  58.8 4.0 %lists_and_loads.1 = (bf16[1024,1536]{1,0:T(8,128)(2,1)}, bf16[1536,1024]{1,0:T(8,128)(2,1)}, f32[1536,128]{1,0:T(8,128)S(1)}, bf16[96,1536]{1,0:T(8,128)(2,1)S(...) custom-call(s32[1,1024]{1,0:T(1,128)S(1)} %bitcast.53, ...), custom_call_target="tpu_custom_call" | custom-call | bytes 8388608 | tf_op jit(solution)/shard_map/lists_and_loads/pallas_call | solution.py:29
  63.0 5.3 %collective-permute-start.1 = (f32[256,128]{1,0:T(8,128)S(1)}, f32[256,128]{1,0:T(8,128)S(1)}, u32[]{:S(2)}, u32[]{:S(2)}) collective-permute-start(f32[256,128]{1,0:T(8,128)S(1)} %get-tuple-element.78), channel_id=1, source_target_pairs={{0,31},{1,2},{2,1},{3,4},{4,3},{5,6},{6,5},{7,8},{8,7},{9,10},{10,... | collective-permute-start | bytes 393224 | tf_op jit(solution)/shard_map/ppermute | solution.py:375
  69.3 5.9 %collective-permute-done.1.a1 = f32[256,128]{1,0:T(8,128)S(1)} collective-permute-done((f32[256,128]{1,0:T(8,128)S(1)}, f32[256,128]{1,0:T(8,128)S(1)}, u32[]{:S(2)}, u32[]{:S(2)}) %collective-permute-start.1) | collective-permute-done | bytes 131104 | tf_op jit(solution)/shard_map/ppermute | solution.py:375
  78.2 6.6 %residual_and_terms.1 = (f32[1536,128]{1,0:T(8,128)S(1)}, f32[1536,128]{1,0:T(8,128)S(1)}, f32[896,128]{1,0:T(8,128)S(1)}) custom-call(f32[1536,128]{1,0:T(8,128)S(1)} %bitcast.41, f32[256,128]{1,0:T(8,128)S(1)} %collective-permute-done.a0, f32[256,128]{1,0:T(8,128)S(1)} %collective-permute-done.1.a1, f32[256,128]{1,0:T(8,128)S(1)} %collective-permute-done.2.a2, ...), custom_call_target="tpu_custom_call" | custom-call | bytes 8388608 | tf_op jit(solution)/shard_map/residual_and_terms/pallas_call | solution.py:29
  87.1 7.0 %all-to-all-start = ((f32[16,56,128]{2,1,0:T(8,128)}), f32[16,56,128]{2,1,0:T(8,128)S(1)}, u32[]{:S(2)}, u32[]{:S(2)}) async-start(f32[16,56,128]{2,1,0:T(8,128)} %bitcast.49), calls=%async_computation | async-start | bytes 917504 | tf_op jit(solution)/shard_map/all_to_all | solution.py:457
  94.3 4.1 %coarse_block.1 = (f32[48,768]{1,0:T(8,128)S(1)}, f32[48,768]{1,0:T(8,128)S(1)}) custom-call(s32[1536]{0:T(1024)S(1)} %reshape.34.map_ref, s32[1]{0:T(128)} %bitcast.12.which_ref, f32[1536,128]{1,0:T(8,128)} %bitcast.14.got_ref), custom_call_target="tpu_custom_call" | custom-call | bytes 8388608 | tf_op jit(solution)/shard_map/coarse_block/pallas_call | solution.py:29
  99.9 8.1 %all-to-all-done = f32[16,56,128]{2,1,0:T(8,128)S(1)} async-done(((f32[16,56,128]{2,1,0:T(8,128)}), f32[16,56,128]{2,1,0:T(8,128)S(1)}, u32[]{:S(2)}, u32[]{:S(2)}) %all-to-all-start) | async-done | bytes 458784 | tf_op jit(solution)/shard_map/all_to_all | solution.py:457
  118.6 3.9 %collective-permute-done.7.a1 = f32[256,128]{1,0:T(8,128)S(1)} collective-permute-done((f32[256,128]{1,0:T(8,128)S(1)}, f32[256,128]{1,0:T(8,128)S(1)}, u32[]{:S(2)}, u32[]{:S(2)}) %collective-permute-start.7) | collective-permute-done | bytes 131104 | tf_op jit(solution)/shard_map/ppermute | solution.py:375
  125.2 7.6 %operator.3 = (f32[1536,128]{1,0:T(8,128)S(1)}, f32[1536,128]{1,0:T(8,128)S(1)}, f32[256,128]{1,0:T(8,128)S(1)}, f32[256,128]{1,0:T(8,128)S(1)}, f32[256,128]{1,0:T(8,128)S(1)}, /*index=5*/f32[256,128]{1,0:T(8,128)S(1)}) custom-call(f32[1536,128]{1,0:T(8,128)S(1)} %get-tuple-element.92.part_ref, f32[256,128]{1,0:T(8,128)S(1)} %collective-permute-done.6.a0, ...), custom_call_target="tpu_custom_call" | custom-call | bytes 8388608 | tf_op jit(solution)/shard_map/operator/pallas_call | solution.py:29
  144.3 6.6 %start.1 = (f32[1536,128]{1,0:T(8,128)S(1)}, f32[1536,128]{1,0:T(8,128)S(1)}, f32[896,128]{1,0:T(8,128)S(1)}) custom-call(f32[1536,128]{1,0:T(8,128)S(1)} %get-tuple-element.97.part_ref, f32[256,128]{1,0:T(8,128)S(1)} %collective-permute-done.10.a0, f32[256,128]{1,0:T(8,128)S(1)} %collective-permute-done.11.a1, f32[256,128]{1,0:T(8,128)S(1)} %collective-permute-done.12.a2, ...), custom_call_target="tpu_custom_call" | custom-call | bytes 8388608 | tf_op jit(solution)/shard_map/start/pallas_call | solution.py:29
  151.9 18.4 %all_to_all.55 = f32[16,56,128]{2,1,0:T(8,128)S(1)} all-to-all(f32[16,56,128]{2,1,0:T(8,128)S(1)} %bitcast.51), channel_id=1, replica_groups={{0,2,4,6,8,10,12,14,16,18,20,22,24,26,28,30},{1,3,5,7,9,11,13,15,17,19,..., dimensions={0} | all-to-all | bytes 917504 | tf_op jit(solution)/shard_map/all_to_all | solution.py:457
  179.5 3.9 %collective-permute-done.16.a1 = f32[256,128]{1,0:T(8,128)S(1)} collective-permute-done((f32[256,128]{1,0:T(8,128)S(1)}, f32[256,128]{1,0:T(8,128)S(1)}, u32[]{:S(2)}, u32[]{:S(2)}) %collective-permute-start.16) | collective-permute-done | bytes 131104 | tf_op jit(solution)/shard_map/ppermute | solution.py:375
  186.1 7.6 %operator.4 = (f32[1536,128]{1,0:T(8,128)S(1)}, f32[1536,128]{1,0:T(8,128)S(1)}, f32[256,128]{1,0:T(8,128)S(1)}, f32[256,128]{1,0:T(8,128)S(1)}, f32[256,128]{1,0:T(8,128)S(1)}, /*index=5*/f32[256,128]{1,0:T(8,128)S(1)}) custom-call(f32[1536,128]{1,0:T(8,128)S(1)} %get-tuple-element.109.part_ref, f32[256,128]{1,0:T(8,128)S(1)} %collective-permute-done.15.a0, ...), custom_call_target="tpu_custom_call" | custom-call | bytes 8388608 | tf_op jit(solution)/shard_map/operator/pallas_call | solution.py:29
  206.8 8.1 %first_update.1 = (f32[1536,128]{1,0:T(8,128)S(1)}, f32[1536,128]{1,0:T(8,128)S(1)}, f32[1536,128]{1,0:T(8,128)S(1)}, f32[1536,128]{1,0:T(8,128)S(1)}, f32[1536,...) custom-call(f32[1536,128]{1,0:T(8,128)} %copy-done.25, ...), custom_call_target="tpu_custom_call" | custom-call | bytes 8388608 | tf_op jit(solution)/shard_map/first_update/pallas_call | solution.py:29
  216.7 18.4 %all_to_all.56 = f32[16,56,128]{2,1,0:T(8,128)S(1)} all-to-all(f32[16,56,128]{2,1,0:T(8,128)S(1)} %bitcast.50), channel_id=1, replica_groups={{0,2,4,6,8,10,12,14,16,18,20,22,24,26,28,30},{1,3,5,7,9,11,13,15,17,19,..., dimensions={0} | all-to-all | bytes 917504 | tf_op jit(solution)/shard_map/all_to_all | solution.py:457
  244.3 3.9 %collective-permute-done.25.a1 = f32[256,128]{1,0:T(8,128)S(1)} collective-permute-done((f32[256,128]{1,0:T(8,128)S(1)}, f32[256,128]{1,0:T(8,128)S(1)}, u32[]{:S(2)}, u32[]{:S(2)}) %collective-permute-start.25) | collective-permute-done | bytes 131104 | tf_op jit(solution)/shard_map/ppermute | solution.py:375
  250.9 8.0 %operator.5 = (f32[1536,128]{1,0:T(8,128)S(1)}, f32[1536,128]{1,0:T(8,128)S(1)}, f32[256,128]{1,0:T(8,128)}, f32[256,128]{1,0:T(8,128)S(1)}, f32[256,128]{1,0:T(8,128)S(1)}, /*index=5*/f32[256,128]{1,0:T(8,128)S(1)}) custom-call(f32[1536,128]{1,0:T(8,128)S(1)} %get-tuple-element.131.part_ref, f32[256,128]{1,0:T(8,128)S(1)} %collective-permute-done.24.a0, ...), custom_call_target="tpu_custom_call" | custom-call | bytes 8388608 | tf_op jit(solution)/shard_map/operator/pallas_call | solution.py:29
  261.4 5.4 %second_update.1 = (f32[1536,128]{1,0:T(8,128)S(1)}, f32[1536,128]{1,0:T(8,128)S(1)}, f32[1536,128]{1,0:T(8,128)S(1)}, f32[1536,128]{1,0:T(8,128)S(1)}, f32[1536...) custom-call(f32[8,128]{1,0:T(8,128)S(1)} %get-tuple-element.108.scal_ref.before_ref, ...), custom_call_target="tpu_custom_call" | custom-call | bytes 8388608 | tf_op jit(solution)/shard_map/second_update/pallas_call | solution.py:29
  273.4 5.3 %collective-permute-start.29 = (f32[256,128]{1,0:T(8,128)}, f32[256,128]{1,0:T(8,128)S(1)}, u32[]{:S(2)}, u32[]{:S(2)}) collective-permute-start(f32[256,128]{1,0:T(8,128)} %copy-done.36), channel_id=1, source_target_pairs={{0,31},{1,2},{2,1},{3,4},{4,3},{5,6},{6,5},{7,8},{8,7},{9,10},{10,... | collective-permute-start | bytes 393224 | tf_op jit(solution)/shard_map/ppermute | solution.py:375
  279.8 4.3 %collective-permute-done.29.a1 = f32[256,128]{1,0:T(8,128)S(1)} collective-permute-done((f32[256,128]{1,0:T(8,128)}, f32[256,128]{1,0:T(8,128)S(1)}, u32[]{:S(2)}, u32[]{:S(2)}) %collective-permute-start.29) | collective-permute-done | bytes 131104 | tf_op jit(solution)/shard_map/ppermute | solution.py:375
  292.9 4.0 %last_update.1 = (f32[1536,128]{1,0:T(8,128)}, f32[1536,128]{1,0:T(8,128)}) custom-call(f32[8,128]{1,0:T(8,128)S(1)} %get-tuple-element.138.state_ref, f32[256,128]{1,0:T(8,128)S(1)} %bitcast.48, f32[1536,128]{1,0:T(8,128)S(1)} %copy-done.7, f32[256,128]{1,0:T(8,128)S(1)} %collective-permute-done.28.a0, f32[256,128]{1,0:T(8,128)S(1)} %collective-permute-done.29.a1, ...), custom_call_target="tpu_custom_call" | custom-call | bytes 8388608 | tf_op jit(solution)/shard_map/last_update/pallas_call | solution.py:29
  (159 shorter events, 98.6 us)
Async XLA Ops:
  49.3 37.9 %all-to-all-start.1 = ((f32[32,48,128]{2,1,0:T(8,128)}), f32[32,48,128]{2,1,0:T(8,128)}, u32[]{:S(2)}, u32[]{:S(2)}) async-start(f32[32,48,128]{2,1,0:T(8,128)} %bitcast.13), calls=%async_computation.1 | async-start | bytes 1572864 | tf_op jit(solution)/shard_map/all_to_all | solution.py:438
  62.8 6.6 %collective-permute-start = (f32[256,128]{1,0:T(8,128)S(1)}, f32[256,128]{1,0:T(8,128)S(1)}, u32[]{:S(2)}, u32[]{:S(2)}) collective-permute-start(f32[256,128]{1,0:T(8,128)S(1)} %get-tuple-element.77), channel_id=1, source_target_pairs={{0,1},{1,0},{2,3},{3,2},{4,5},{5,4},{6,7},{7,6},{8,9},{9,8},{10,11... | collective-permute-start | bytes 393224 | tf_op jit(solution)/shard_map/ppermute | solution.py:375
  63.0 12.3 %collective-permute-start.1 = (f32[256,128]{1,0:T(8,128)S(1)}, f32[256,128]{1,0:T(8,128)S(1)}, u32[]{:S(2)}, u32[]{:S(2)}) collective-permute-start(f32[256,128]{1,0:T(8,128)S(1)} %get-tuple-element.78), channel_id=1, source_target_pairs={{0,31},{1,2},{2,1},{3,4},{4,3},{5,6},{6,5},{7,8},{8,7},{9,10},{10,... | collective-permute-start | bytes 393224 | tf_op jit(solution)/shard_map/ppermute | solution.py:375
  68.3 8.1 %collective-permute-start.2 = (f32[256,128]{1,0:T(8,128)S(1)}, f32[256,128]{1,0:T(8,128)S(1)}, u32[]{:S(2)}, u32[]{:S(2)}) collective-permute-start(f32[256,128]{1,0:T(8,128)S(1)} %get-tuple-element.79), channel_id=1, source_target_pairs={{0,8},{1,9},{2,10},{3,11},{4,12},{5,13},{6,14},{7,15},{8,0},{9,1},... | collective-permute-start | bytes 393224 | tf_op jit(solution)/shard_map/ppermute | solution.py:375
  68.3 9.9 %collective-permute-start.3 = (f32[256,128]{1,0:T(8,128)S(1)}, f32[256,128]{1,0:T(8,128)S(1)}, u32[]{:S(2)}, u32[]{:S(2)}) collective-permute-start(f32[256,128]{1,0:T(8,128)S(1)} %get-tuple-element.80), channel_id=1, source_target_pairs={{0,24},{1,25},{2,26},{3,27},{4,28},{5,29},{6,30},{7,31},{8,16},{9,... | collective-permute-start | bytes 393224 | tf_op jit(solution)/shard_map/ppermute | solution.py:375
  87.1 20.8 %all-to-all-start = ((f32[16,56,128]{2,1,0:T(8,128)}), f32[16,56,128]{2,1,0:T(8,128)S(1)}, u32[]{:S(2)}, u32[]{:S(2)}) async-start(f32[16,56,128]{2,1,0:T(8,128)} %bitcast.49), calls=%async_computation | async-start | bytes 917504 | tf_op jit(solution)/shard_map/all_to_all | solution.py:457
  114.3 8.3 %collective-permute-start.7 = (f32[256,128]{1,0:T(8,128)S(1)}, f32[256,128]{1,0:T(8,128)S(1)}, u32[]{:S(2)}, u32[]{:S(2)}) collective-permute-start(f32[256,128]{1,0:T(8,128)S(1)} %get-tuple-element.94), channel_id=1, source_target_pairs={{0,31},{1,2},{2,1},{3,4},{4,3},{5,6},{6,5},{7,8},{8,7},{9,10},{10,... | collective-permute-start | bytes 393224 | tf_op jit(solution)/shard_map/ppermute | solution.py:375
  116.6 6.0 %collective-permute-start.8 = (f32[256,128]{1,0:T(8,128)S(1)}, f32[256,128]{1,0:T(8,128)S(1)}, u32[]{:S(2)}, u32[]{:S(2)}) collective-permute-start(f32[256,128]{1,0:T(8,128)S(1)} %get-tuple-element.95), channel_id=1, source_target_pairs={{0,8},{1,9},{2,10},{3,11},{4,12},{5,13},{6,14},{7,15},{8,0},{9,1},... | collective-permute-start | bytes 393224 | tf_op jit(solution)/shard_map/ppermute | solution.py:375
  116.6 8.6 %collective-permute-start.9 = (f32[256,128]{1,0:T(8,128)S(1)}, f32[256,128]{1,0:T(8,128)S(1)}, u32[]{:S(2)}, u32[]{:S(2)}) collective-permute-start(f32[256,128]{1,0:T(8,128)S(1)} %get-tuple-element.96), channel_id=1, source_target_pairs={{0,24},{1,25},{2,26},{3,27},{4,28},{5,29},{6,30},{7,31},{8,16},{9,... | collective-permute-start | bytes 393224 | tf_op jit(solution)/shard_map/ppermute | solution.py:375
  132.8 6.4 %collective-permute-start.10 = (f32[256,128]{1,0:T(8,128)S(1)}, f32[256,128]{1,0:T(8,128)S(1)}, u32[]{:S(2)}, u32[]{:S(2)}) collective-permute-start(f32[256,128]{1,0:T(8,128)S(1)} %get-tuple-element.98), channel_id=1, source_target_pairs={{0,1},{1,0},{2,3},{3,2},{4,5},{5,4},{6,7},{7,6},{8,9},{9,8},{10,11... | collective-permute-start | bytes 393224 | tf_op jit(solution)/shard_map/ppermute | solution.py:375
  132.9 8.4 %collective-permute-start.11 = (f32[256,128]{1,0:T(8,128)S(1)}, f32[256,128]{1,0:T(8,128)S(1)}, u32[]{:S(2)}, u32[]{:S(2)}) collective-permute-start(f32[256,128]{1,0:T(8,128)S(1)} %get-tuple-element.99), channel_id=1, source_target_pairs={{0,31},{1,2},{2,1},{3,4},{4,3},{5,6},{6,5},{7,8},{8,7},{9,10},{10,... | collective-permute-start | bytes 393224 | tf_op jit(solution)/shard_map/ppermute | solution.py:375
  136.2 8.1 %collective-permute-start.13 = (f32[256,128]{1,0:T(8,128)S(1)}, f32[256,128]{1,0:T(8,128)S(1)}, u32[]{:S(2)}, u32[]{:S(2)}) collective-permute-start(f32[256,128]{1,0:T(8,128)S(1)} %get-tuple-element.101), channel_id=1, source_target_pairs={{0,24},{1,25},{2,26},{3,27},{4,28},{5,29},{6,30},{7,31},{8,16},{9,... | collective-permute-start | bytes 393224 | tf_op jit(solution)/shard_map/ppermute | solution.py:375
  175.1 8.3 %collective-permute-start.16 = (f32[256,128]{1,0:T(8,128)S(1)}, f32[256,128]{1,0:T(8,128)S(1)}, u32[]{:S(2)}, u32[]{:S(2)}) collective-permute-start(f32[256,128]{1,0:T(8,128)S(1)} %get-tuple-element.111), channel_id=1, source_target_pairs={{0,31},{1,2},{2,1},{3,4},{4,3},{5,6},{6,5},{7,8},{8,7},{9,10},{10,... | collective-permute-start | bytes 393224 | tf_op jit(solution)/shard_map/ppermute | solution.py:375
  177.5 8.6 %collective-permute-start.18 = (f32[256,128]{1,0:T(8,128)S(1)}, f32[256,128]{1,0:T(8,128)S(1)}, u32[]{:S(2)}, u32[]{:S(2)}) collective-permute-start(f32[256,128]{1,0:T(8,128)S(1)} %get-tuple-element.113), channel_id=1, source_target_pairs={{0,24},{1,25},{2,26},{3,27},{4,28},{5,29},{6,30},{7,31},{8,16},{9,... | collective-permute-start | bytes 393224 | tf_op jit(solution)/shard_map/ppermute | solution.py:375
  195.4 6.3 %collective-permute-start.19 = (f32[256,128]{1,0:T(8,128)S(1)}, f32[256,128]{1,0:T(8,128)S(1)}, u32[]{:S(2)}, u32[]{:S(2)}) collective-permute-start(f32[256,128]{1,0:T(8,128)S(1)} %get-tuple-element.115), channel_id=1, source_target_pairs={{0,1},{1,0},{2,3},{3,2},{4,5},{5,4},{6,7},{7,6},{8,9},{9,8},{10,11... | collective-permute-start | bytes 393224 | tf_op jit(solution)/shard_map/ppermute | solution.py:375
  195.4 8.4 %collective-permute-start.20 = (f32[256,128]{1,0:T(8,128)S(1)}, f32[256,128]{1,0:T(8,128)S(1)}, u32[]{:S(2)}, u32[]{:S(2)}) collective-permute-start(f32[256,128]{1,0:T(8,128)S(1)} %get-tuple-element.116), channel_id=1, source_target_pairs={{0,31},{1,2},{2,1},{3,4},{4,3},{5,6},{6,5},{7,8},{8,7},{9,10},{10,... | collective-permute-start | bytes 393224 | tf_op jit(solution)/shard_map/ppermute | solution.py:375
  198.7 8.1 %collective-permute-start.22 = (f32[256,128]{1,0:T(8,128)S(1)}, f32[256,128]{1,0:T(8,128)S(1)}, u32[]{:S(2)}, u32[]{:S(2)}) collective-permute-start(f32[256,128]{1,0:T(8,128)S(1)} %get-tuple-element.118), channel_id=1, source_target_pairs={{0,24},{1,25},{2,26},{3,27},{4,28},{5,29},{6,30},{7,31},{8,16},{9,... | collective-permute-start | bytes 393224 | tf_op jit(solution)/shard_map/ppermute | solution.py:375
  240.0 8.3 %collective-permute-start.25 = (f32[256,128]{1,0:T(8,128)S(1)}, f32[256,128]{1,0:T(8,128)S(1)}, u32[]{:S(2)}, u32[]{:S(2)}) collective-permute-start(f32[256,128]{1,0:T(8,128)S(1)} %get-tuple-element.133), channel_id=1, source_target_pairs={{0,31},{1,2},{2,1},{3,4},{4,3},{5,6},{6,5},{7,8},{8,7},{9,10},{10,... | collective-permute-start | bytes 393224 | tf_op jit(solution)/shard_map/ppermute | solution.py:375
  242.3 8.6 %collective-permute-start.27 = (f32[256,128]{1,0:T(8,128)S(1)}, f32[256,128]{1,0:T(8,128)S(1)}, u32[]{:S(2)}, u32[]{:S(2)}) collective-permute-start(f32[256,128]{1,0:T(8,128)S(1)} %get-tuple-element.135), channel_id=1, source_target_pairs={{0,24},{1,25},{2,26},{3,27},{4,28},{5,29},{6,30},{7,31},{8,16},{9,... | collective-permute-start | bytes 393224 | tf_op jit(solution)/shard_map/ppermute | solution.py:375
  269.5 18.2 %all-to-all-start.4 = ((f32[32,8,128]{2,1,0:T(8,128)}), f32[32,8,128]{2,1,0:T(8,128)S(1)}, u32[]{:S(2)}, u32[]{:S(2)}) async-start(f32[32,8,128]{2,1,0:T(8,128)} %bitcast.20), calls=%async_computation.4 | async-start | bytes 262144 | tf_op jit(solution)/shard_map/all_to_all | solution.py:508
  273.1 6.7 %collective-permute-start.28 = (f32[256,128]{1,0:T(8,128)}, f32[256,128]{1,0:T(8,128)S(1)}, u32[]{:S(2)}, u32[]{:S(2)}) collective-permute-start(f32[256,128]{1,0:T(8,128)} %get-tuple-element.140), channel_id=1, source_target_pairs={{0,1},{1,0},{2,3},{3,2},{4,5},{5,4},{6,7},{7,6},{8,9},{9,8},{10,11... | collective-permute-start | bytes 393224 | tf_op jit(solution)/shard_map/ppermute | solution.py:375
  273.4 10.7 %collective-permute-start.29 = (f32[256,128]{1,0:T(8,128)}, f32[256,128]{1,0:T(8,128)S(1)}, u32[]{:S(2)}, u32[]{:S(2)}) collective-permute-start(f32[256,128]{1,0:T(8,128)} %copy-done.36), channel_id=1, source_target_pairs={{0,31},{1,2},{2,1},{3,4},{4,3},{5,6},{6,5},{7,8},{8,7},{9,10},{10,... | collective-permute-start | bytes 393224 | tf_op jit(solution)/shard_map/ppermute | solution.py:375
  278.8 6.1 %collective-permute-start.30 = (f32[256,128]{1,0:T(8,128)}, f32[256,128]{1,0:T(8,128)S(1)}, u32[]{:S(2)}, u32[]{:S(2)}) collective-permute-start(f32[256,128]{1,0:T(8,128)} %copy-done.35), channel_id=1, source_target_pairs={{0,8},{1,9},{2,10},{3,11},{4,12},{5,13},{6,14},{7,15},{8,0},{9,1},... | collective-permute-start | bytes 393224 | tf_op jit(solution)/shard_map/ppermute | solution.py:375
  278.8 8.3 %collective-permute-start.31 = (f32[256,128]{1,0:T(8,128)}, f32[256,128]{1,0:T(8,128)S(1)}, u32[]{:S(2)}, u32[]{:S(2)}) collective-permute-start(f32[256,128]{1,0:T(8,128)} %copy-done.34), channel_id=1, source_target_pairs={{0,24},{1,25},{2,26},{3,27},{4,28},{5,29},{6,30},{7,31},{8,16},{9,... | collective-permute-start | bytes 393224 | tf_op jit(solution)/shard_map/ppermute | solution.py:375
  (50 other events, 507.7 us)

commit v2 on v1

--- a/solution.py
+++ b/solution.py
@@ -10,18 +10,32 @@
 BF16 = jnp.bfloat16
 TILE = 512
 SCAL = 8
+ORDER = (3, 1, 2, 0)
 LANES = 128
 
 VSPEC = pl.BlockSpec(memory_space=pltpu.VMEM)
 SSPEC = pl.BlockSpec(memory_space=pltpu.SMEM)
+ASPEC = pl.BlockSpec(memory_space=pl.ANY)
 
 
 def near(shape, dtype=F32):
-    return jax.ShapeDtypeStruct(shape, dtype)
+    return pltpu.VMEM(shape, dtype)
 
 
 def far(shape, dtype=F32):
     return jax.ShapeDtypeStruct(shape, dtype)
+
+
+def away(shape, dtype=F32):
+    return pltpu.HBM(shape, dtype)
+
+
+def held(*arrays):
+    return tuple(pltpu.with_memory_space_constraint(a, pltpu.VMEM) for a in arrays)
+
+
+def aside(*arrays):
+    return tuple(pltpu.with_memory_space_constraint(a, pltpu.HBM) for a in arrays)
 
 
 def call(kernel, name, args, outs, scratch=(), specs=None, flops=0):
@@ -33,7 +47,7 @@
         in_specs=[specs.get(i, VSPEC) for i in range(len(args))],
         out_specs=tuple(VSPEC for _ in outs),
         scratch_shapes=list(scratch),
-        compiler_params=pltpu.CompilerParams(vmem_limit_bytes=48 * 1024 * 1024),
+        compiler_params=pltpu.CompilerParams(vmem_limit_bytes=20 * 1024 * 1024),
         cost_estimate=pl.CostEstimate(
             flops=flops, bytes_accessed=8 * 1024 * 1024, transcendentals=0
         ),
@@ -84,28 +98,65 @@
         arr_cat[j * cap : (j + 1) * cap, :] = pair(ref[...])
 
 
-def setup_kernel(row_ref, col_ref, count_ref, basis_ref, basis_t_ref, loads_ref,
-                 pick_ref, place_ref, weight_ref, basis2_ref, basis3_ref,
-                 out0, out1, out2, out3, cat):
+def fill_pick(row_ref, pick_ref):
     slots, rows = pick_ref.shape
-    rhs = loads_ref.shape[1]
+    entries = jnp.broadcast_to(row_ref[...].astype(F32), (LANES, slots)).T
     for lo, n in tiles(slots):
-        at = lax.broadcasted_iota(jnp.int32, (n, rows), 1)
-        pick_ref[lo : lo + n, :] = jnp.where(at == col_ref[lo : lo + n, :], 1.0, 0.0).astype(BF16)
-    for lo, n in tiles(rows):
-        cat[lo : lo + n, :] = pair(loads_ref[lo : lo + n, :])
-    pick_out(pick_ref, cat, (out0, out1, out2, out3))
+        for left in range(0, rows, LANES):
+            at = left + lax.broadcasted_iota(jnp.int32, (n, LANES), 1)
+            same = at.astype(F32) == entries[lo : lo + n]
+            pick_ref[lo : lo + n, left : left + LANES] = jnp.where(same, 1.0, 0.0).astype(BF16)
+
+
+def fill_place(row_ref, place_ref):
+    rows, slots = place_ref.shape
     for lo, n in tiles(rows):
         at = lo + lax.broadcasted_iota(jnp.int32, (n, slots), 0)
         place_ref[lo : lo + n, :] = jnp.where(at == row_ref[...], 1.0, 0.0).astype(BF16)
-        weight = 1.0 / count_ref[lo : lo + n, :].astype(F32)
-        weight_ref[lo : lo + n, :] = jnp.broadcast_to(weight, (n, rhs))
+
+
+def weights_of(count_ref):
+    rows = count_ref.shape[1]
+    return jnp.broadcast_to(1.0 / count_ref[...].astype(F32), (LANES, rows)).T
+
+
+def fill_basis2(basis_ref, basis2_ref):
     ncl = basis_ref.shape[0]
     high, low = cut(basis_ref[...])
     basis2_ref[:ncl, :] = high
     basis2_ref[ncl:, :] = low
-    high, low = cut(basis_t_ref[...])
-    basis3_ref[...] = jnp.concatenate([high, high, low], axis=1)
+
+
+def loads_kernel(row_ref, loads_ref, out0, out1, out2, out3, pick, cat):
+    fill_pick(row_ref, pick)
+    for lo, n in tiles(loads_ref.shape[0]):
+        cat[lo : lo + n, :] = pair(loads_ref[lo : lo + n, :])
+    pick_out(pick, cat, (out0, out1, out2, out3))
+
+
+def back_tables_kernel(row_ref, count_ref, basis_ref, after_ref,
+                       pick_ref, weight_ref, basis3_ref):
+    fill_pick(row_ref, pick_ref)
+    weight_ref[...] = weights_of(count_ref)
+    ncl, rows = basis_ref.shape
+    high, low = cut(basis_ref[...])
+    high, low = high.astype(F32), low.astype(F32)
+    fill = jnp.zeros((basis3_ref.shape[1] - 3 * ncl, rows), F32)
+    basis3_ref[...] = jnp.concatenate([high, high, low, fill], axis=0).T.astype(BF16)
+
+
+def tables_kernel(row_ref, basis_ref, stiff_from, inverse_from, after_ref,
+                  place_ref, basis2_ref, stiff_ref, inverse_ref, sems):
+    copies = [
+        pltpu.make_async_copy(stiff_from, stiff_ref, sems.at[0]),
+        pltpu.make_async_copy(inverse_from, inverse_ref, sems.at[1]),
+    ]
+    for copy in copies:
+        copy.start()
+    fill_place(row_ref, place_ref)
+    fill_basis2(basis_ref, basis2_ref)
+    for copy in copies:
+        copy.wait()
 
 
 def columns_kernel(map_ref, inverse_ref, out_ref, turned):
@@ -113,13 +164,15 @@
     for lo, n in tiles(order):
         turned[lo : lo + n, :] = inverse_ref[:, lo : lo + n].T
 
+    size = map_ref.shape[0]
+    ncl = out_ref.shape[0] // size
+
     def step(i, _):
-        for k in range(8):
-            m = i * 8 + k
-            out_ref[pl.ds(m, 1), :] = turned[pl.ds(map_ref[m], 1), :]
+        for k in range(ncl):
+            out_ref[pl.ds(i * ncl + k, 1), :] = turned[pl.ds(map_ref[i, k], 1), :]
         return 0
 
-    lax.fori_loop(0, out_ref.shape[0] // 8, step, 0)
+    lax.fori_loop(0, size, step, 0)
 
 
 def coarse_kernel(map_ref, which_ref, got_ref, keep_ref, send_ref, turned, rowed):
@@ -130,13 +183,16 @@
         block = jnp.concatenate([got_ref[t * ncl : (t + 1) * ncl, :], fill], axis=0)
         turned[t * width : (t + 1) * width, :] = block.T
 
+    size = map_ref.shape[0]
+
     def step(i, _):
-        for k in range(8):
-            m = i * 8 + k
-            rowed[pl.ds(m, 1), :] = turned[pl.ds(map_ref[m], 1), :]
+        for c in range(2):
+            for k in range(ncl):
+                row = turned[pl.ds(map_ref[2 * i + c, k], 1), :]
+                rowed[pl.ds(c * half + i * ncl + k, 1), :] = row
         return 0
 
-    lax.fori_loop(0, rowed.shape[0] // 8, step, 0)
+    lax.fori_loop(0, size // 2, step, 0)
     first = rowed[:half, :].T[:ncl, :]
     second = rowed[half:, :].T[:ncl, :]
     even = which_ref[0] == 0
@@ -144,7 +200,8 @@
     send_ref[...] = jnp.where(even, second, first)
 
 
-def stack_kernel(own_ref, other_ref, out_ref):
+def stack_kernel(own_ref, other_ref, terms_ref, out_ref, after_ref):
+    after_ref[...] = jnp.zeros_like(after_ref)
     ncl = own_ref.shape[0]
     own_high, own_low = cut(own_ref[...])
     other_high, other_low = cut(other_ref[...])
@@ -166,21 +223,27 @@
         local_ref[lo : lo + n, :] = halves(dot(inverse_ref[lo : lo + n, :], cat[...]))
 
 
-def first_kernel(loads_ref, a0, a1, a2, a3, place_ref, weight_ref, basis2_ref, inverse_ref,
-                 resid_ref, local_ref, send_ref, cat, arr_cat):
-    ncl = basis2_ref.shape[0] // 2
-    rhs = loads_ref.shape[1]
+def first_kernel(loads_ref, a0, a1, a2, a3, row_ref, count_ref, basis_ref, inverse_from,
+                 resid_ref, local_ref, send_ref,
+                 cat, arr_cat, place, basis2, inverse, weight, sems):
+    copy = pltpu.make_async_copy(inverse_from, inverse, sems.at[0])
+    copy.start()
+    fill_place(row_ref, place)
+    fill_basis2(basis_ref, basis2)
+    weight[...] = weights_of(count_ref)
+    ncl, rhs = basis_ref.shape[0], loads_ref.shape[1]
     arrivals((a0, a1, a2, a3), arr_cat)
     terms = jnp.zeros((2 * ncl, 2 * rhs), F32)
     for lo, n in tiles(loads_ref.shape[0]):
         at = slice(lo, lo + n)
-        resid = loads_ref[at, :] + halves(dot(place_ref[at, :], arr_cat[...]))
+        resid = loads_ref[at, :] + halves(dot(place[at, :], arr_cat[...]))
         resid_ref[at, :] = resid
-        both = pair(weight_ref[at, :] * resid)
+        both = pair(weight[at, :] * resid)
         cat[at, :] = both
-        terms += dot(basis2_ref[:, at], both)
+        terms += dot(basis2[:, at], both)
     send_terms(three(terms, ncl), jnp.zeros((SCAL, rhs), F32), send_ref)
-    front(inverse_ref, cat, local_ref)
+    copy.wait()
+    front(inverse, cat, local_ref)
 
 
 def coarse_solve_kernel(got_ref, g_ref, own_ref, other_ref):
@@ -203,7 +266,8 @@
     total = own_ref[...] + other_ref[...]
     scal_ref[...] = total[ncl:]
     high, low = cut(total[:ncl])
-    values = jnp.concatenate([high, low, high], axis=0)
+    fill = jnp.zeros((basis3_ref.shape[1] - 3 * ncl, high.shape[1]), BF16)
+    values = jnp.concatenate([high, low, high, fill], axis=0)
     for lo, n in tiles(local_ref.shape[0]):
         at = slice(lo, lo + n)
         field = weight_ref[at, :] * (local_ref[at, :] + dot(basis3_ref[at, :], values))
@@ -299,9 +363,14 @@
     return beta, now[0:1, :] / energy, energy
 
 
-def third_kernel(before_ref, scal_ref, x1_ref, r1_ref, u1_ref, w1_ref, p_ref, s_ref, q_ref, z_ref,
-                 m_ref, image_ref, weight_ref,
-                 x2_ref, r2_ref, u2_ref, half_ref, p1_ref, s1_ref, state_ref, send_ref):
+def third_kernel(part_ref, a0, a1, a2, a3, place_ref, stiff_ref, pick_ref,
+                 before_ref, scal_ref, x1_ref, r1_ref, u1_ref, w1_ref, p_ref, s_ref, q_ref, z_ref,
+                 weight_ref,
+                 out0, out1, out2, out3, send_ref, state_ref,
+                 x2_ref, r2_ref, u2_ref, half_ref, p1_ref, s1_ref,
+                 cat, arr_cat, cat2, m, image):
+    apply_kernel(part_ref, a0, a1, a2, a3, place_ref, stiff_ref, pick_ref,
+                 m, image, out0, out1, out2, out3, cat, arr_cat, cat2)
     rhs = r1_ref.shape[1]
     beta, alpha, energy = step_scalars(before_ref[...], scal_ref[...])
     sums = [jnp.zeros((8, rhs), F32) for _ in range(4)]
@@ -309,21 +378,21 @@
         at = slice(lo, lo + n)
         p1 = u1_ref[at, :] + beta * p_ref[at, :]
         s1 = w1_ref[at, :] + beta * s_ref[at, :]
-        q1 = m_ref[at, :] + beta * q_ref[at, :]
+        q1 = m[at, :] + beta * q_ref[at, :]
         r2 = r1_ref[at, :] - alpha * s1
         u2 = u1_ref[at, :] - alpha * q1
         half = w1_ref[at, :] - (alpha * beta) * z_ref[at, :]
+        weight = weight_ref[at, :]
+        left = weight * half - alpha * image[at, :]
+        weighted = weight * u2
+        for k, term in enumerate((weighted * r2, u2 * left, weighted * s1, p1 * left)):
+            sums[k] += folded(term)
         x2_ref[at, :] = x1_ref[at, :] + alpha * p1
         r2_ref[at, :] = r2
         u2_ref[at, :] = u2
-        half_ref[at, :] = half
+        half_ref[at, :] = half - alpha * image[at, :]
         p1_ref[at, :] = p1
         s1_ref[at, :] = s1
-        weight = weight_ref[at, :]
-        left = weight * half - alpha * image_ref[at, :]
-        weighted = weight * u2
-        for k, term in enumerate((weighted * r2, u2 * left, weighted * s1, p1 * left)):
-            sums[k] += folded(term)
     block = collect(sums, rhs)
     for g in range(send_ref.shape[0] // SCAL):
         send_ref[g * SCAL : (g + 1) * SCAL, :] = block
@@ -332,9 +401,10 @@
     )
 
 
-def last_kernel(state_ref, got_ref, image_ref, a0, a1, a2, a3, place_ref,
+def last_kernel(row_ref, state_ref, got_ref, a0, a1, a2, a3,
                 x2_ref, r2_ref, u2_ref, half_ref, p1_ref, s1_ref,
-                x3_ref, r3_ref, arr_cat):
+                x3_ref, r3_ref, place, arr_cat):
+    fill_place(row_ref, place)
     arrivals((a0, a1, a2, a3), arr_cat)
     state = state_ref[...]
     now = jnp.sum(got_ref[...].reshape(-1, SCAL, got_ref.shape[1]), axis=0)
@@ -342,8 +412,7 @@
     old = state[2:3, :]
     for lo, n in tiles(r2_ref.shape[0]):
         at = slice(lo, lo + n)
-        image = image_ref[at, :] + halves(dot(place_ref[at, :], arr_cat[...]))
-        w2 = half_ref[at, :] - old * image
+        w2 = half_ref[at, :] - old * halves(dot(place[at, :], arr_cat[...]))
         x3_ref[at, :] = x2_ref[at, :] + alpha * (u2_ref[at, :] + beta * p1_ref[at, :])
         r3_ref[at, :] = r2_ref[at, :] - alpha * (w2 + beta * s1_ref[at, :])
 
@@ -367,13 +436,12 @@
 
         return [(i, of(i)) for i in range(size)]
 
-    swaps = [partner(1, 0), partner(1, 1), partner(STRIDE, 0), partner(STRIDE, 1)]
+    inside = partner(1, 0)
+    swaps = [inside, partner(1, 1), partner(STRIDE, 0), partner(STRIDE, 1)]
+    swaps = [swaps[j] for j in ORDER]
 
     def exchange(outs):
-        got = [None] * len(outs)
-        for j in (3, 2, 1, 0):
-            got[j] = lax.ppermute(outs[j], "sub", swaps[j])
-        return got
+        return [lax.ppermute(out, "sub", swap) for out, swap in zip(outs, swaps)]
 
     cores = [[2 * i + c for i in range(size // 2)] for c in range(2)]
     groups = size // 2
@@ -390,42 +458,27 @@
         axis=0,
     )
 
-    maps = lax.all_gather(coarse_map[0], "sub", axis=0, tiled=True)
-
     fields = (rows, rhs)
     out4 = [far((cap, rhs))] * 4
     wide = pltpu.VMEM((rows, 2 * rhs), BF16)
     wide_arr = pltpu.VMEM((lists, 2 * rhs), BF16)
-
-    pick, place, weight, basis2, basis3, *outs = call(
-        setup_kernel,
-        "lists_and_loads",
-        (
-            mine.reshape(1, lists),
-            mine.reshape(lists, 1),
-            counts[0].reshape(rows, 1),
-            coarse_basis[0],
-            coarse_basis[0].T,
-            loads[0],
-        ),
-        [
-            near((lists, rows), BF16),
-            near((rows, lists), BF16),
-            near(fields),
-            near((2 * ncl, rows), BF16),
-            near((rows, 3 * ncl), BF16),
-        ]
-        + out4,
-        [wide],
-    )
-    got = exchange(outs)
-    r0, local, send = call(
-        first_kernel,
-        "residual_and_terms",
-        (loads[0], *got, place, weight, basis2, inverse),
-        [near(fields), near(fields), far((groups * block, rhs))],
-        [wide, wide_arr],
-    )
+    place_like = pltpu.VMEM((rows, lists), BF16)
+    listed = jnp.concatenate([mine[j] for j in ORDER]).reshape(1, lists)
+    basis = coarse_basis[0]
+
+    outs = call(
+        loads_kernel,
+        "loads",
+        (listed, loads[0]),
+        out4,
+        [pltpu.VMEM((lists, rows), BF16), wide],
+    )
+    arrived = exchange(outs)
+    own_map = jnp.pad(coarse_map, ((0, 0), (0, -ncl % LANES)))
+    maps = jnp.broadcast_to(own_map, (size, own_map.shape[1]))
+    maps = lax.all_to_all(maps, "sub", 0, 0, tiled=True)
+    maps, *arrived = lax.optimization_barrier((maps, *arrived))
+
 
     (picked,) = call(
         columns_kernel,
@@ -436,11 +489,29 @@
         {0: SSPEC},
     )
     mine_rows = lax.all_to_all(picked, "sub", 0, 0, tiled=True)
-    by_core = maps.reshape(groups, 2, ncl).swapaxes(0, 1).reshape(-1)
+
+    r0, local, send = call(
+        first_kernel,
+        "residual_and_terms",
+        (loads[0], *arrived, listed, counts, basis, inverse),
+        [away(fields), away(fields), far((groups * block, rhs))],
+        [
+            wide,
+            wide_arr,
+            place_like,
+            pltpu.VMEM((2 * ncl, rows), BF16),
+            pltpu.VMEM((rows, rows), BF16),
+            pltpu.VMEM(fields, F32),
+            pltpu.SemaphoreType.DMA((1,)),
+        ],
+        {8: ASPEC},
+    )
+    r0, local = aside(r0, local)
+
     keep, pass_on = call(
         coarse_kernel,
         "coarse_block",
-        (by_core, (me % 2).reshape(1), mine_rows),
+        (maps, (me % 2).reshape(1), mine_rows),
         [far((ncl, groups * ncl)), far((ncl, groups * ncl))],
         [
             pltpu.VMEM((order, LANES), F32),
@@ -448,20 +519,48 @@
         ],
         {0: SSPEC, 1: SSPEC},
     )
-    passed = lax.ppermute(pass_on, "sub", swaps[0])
-    (coarse,) = call(
-        stack_kernel, "coarse_addends", (keep, passed), [near((4 * ncl, groups * ncl), BF16)]
-    )
-
-    def middle(send, local):
-        got = lax.all_to_all(send, "sub", 0, 0, tiled=True, axis_index_groups=cores)
+    passed = lax.ppermute(pass_on, "sub", inside)
+
+    def share(send):
+        return lax.all_to_all(send, "sub", 0, 0, tiled=True, axis_index_groups=cores)
+
+    terms = share(send)
+    coarse, after = call(
+        stack_kernel,
+        "coarse_addends",
+        (keep, passed, terms),
+        [near((4 * ncl, groups * ncl), BF16), far((SCAL, LANES))],
+    )
+    pick, weight, basis3 = call(
+        back_tables_kernel,
+        "back_tables",
+        (listed, counts, basis, after),
+        [near((lists, rows), BF16), near(fields), near((rows, 2 * LANES), BF16)],
+    )
+    place, basis2, stiff, inverse = call(
+        tables_kernel,
+        "tables",
+        (listed, basis, stiff, inverse, after),
+        [
+            near((rows, lists), BF16),
+            near((2 * ncl, rows), BF16),
+            near((rows, rows), BF16),
+            near((rows, rows), BF16),
+        ],
+        [pltpu.SemaphoreType.DMA((2,))],
+        {2: ASPEC, 3: ASPEC},
+    )
+    coarse, pick, weight, basis3 = held(coarse, pick, weight, basis3)
+    place, basis2, stiff, inverse = held(place, basis2, stiff, inverse)
+
+    def correct(terms, local):
         own, other = call(
             coarse_solve_kernel,
             "coarse_solve",
-            (got, coarse),
+            (terms, coarse),
             [far((block, rhs)), far((block, rhs))],
         )
-        came = lax.ppermute(other, "sub", swaps[0])
+        came = lax.ppermute(other, "sub", inside)
         part, scal, *outs = call(
             back_kernel,
             "coarse_back",
@@ -469,7 +568,9 @@
             [near(fields), near((SCAL, rhs))] + out4,
             [wide],
         )
-        arrived = exchange(outs)
+        return *held(part, scal), exchange(outs)
+
+    def operate(part, arrived):
         field, image, *outs = call(
             apply_kernel,
             "operator",
@@ -477,41 +578,46 @@
             [near(fields), near(fields)] + out4,
             [wide, wide_arr, wide],
         )
-        return scal, field, image, outs
-
-    _, u0, image, outs = middle(send, local)
-    got = exchange(outs)
+        return *held(field, image), exchange(outs)
+
+    part, _, arrived = correct(terms, local)
+    u0, image, arrived = operate(part, arrived)
     w0, local, send = call(
         start_kernel,
         "start",
-        (image, *got, r0, u0, place, weight, basis2, inverse),
+        (image, *arrived, r0, u0, place, weight, basis2, inverse),
         [near(fields), near(fields), far((groups * block, rhs))],
         [wide, wide_arr],
     )
-    scal0, m0, image, outs = middle(send, local)
-    got = exchange(outs)
-    z0, x1, r1, u1, w1, local, send = call(
+    w0, local = held(w0, local)
+    part, scal0, arrived = correct(share(send), local)
+    m0, image, arrived = operate(part, arrived)
+    *news, send = call(
         second_kernel,
         "first_update",
-        (image, *got, scal0, r0, u0, w0, m0, place, weight, basis2, inverse),
+        (image, *arrived, scal0, r0, u0, w0, m0, place, weight, basis2, inverse),
         [near(fields)] * 6 + [far((groups * block, rhs))],
         [wide, wide_arr],
     )
-    scal1, m1, image, outs = middle(send, local)
-    got = exchange(outs)
-    x2, r2, u2, half, p1, s1, state, send = call(
+    z0, x1, r1, u1, w1, local = held(*news)
+    part, scal1, arrived = correct(share(send), local)
+    *outs, send, state, x2, r2, u2, half, p1, s1 = call(
         third_kernel,
         "second_update",
-        (scal0, scal1, x1, r1, u1, w1, u0, w0, m0, z0, m1, image, weight),
-        [near(fields)] * 6 + [near((SCAL, rhs)), far((size * SCAL, rhs))],
-    )
+        (part, *arrived, place, stiff, pick)
+        + (scal0, scal1, x1, r1, u1, w1, u0, w0, m0, z0, weight),
+        out4 + [far((size * SCAL, rhs)), far((SCAL, rhs))] + [away(fields)] * 6,
+        [wide, wide_arr, wide, pltpu.VMEM(fields, F32), pltpu.VMEM(fields, F32)],
+    )
+    x2, r2, u2, half, p1, s1 = aside(x2, r2, u2, half, p1, s1)
+    arrived = exchange(outs)
     sums = lax.all_to_all(send, "sub", 0, 0, tiled=True)
     x3, r3 = call(
         last_kernel,
         "last_update",
-        (state, sums, image, *got, place, x2, r2, u2, half, p1, s1),
+        (listed, state, sums, *arrived, x2, r2, u2, half, p1, s1),
         [far(fields), far(fields)],
-        [wide_arr],
+        [place_like, wide_arr],
     )
     return (x3[None], r3[None])
 

time: 298 us -> 216 us (0.72)
  blocking collectives: 78.8 us -> 45 us
  Pallas kernels: 76.7 us -> 45.9 us
  local copies, waits for them, and re-layouts: 27.1 us -> 11.3 us
  starting transfers between devices: 55 us -> 48.3 us
  waiting for transfers between devices: 58.3 us -> 62.8 us
    all_gather x1 -> x0, blocking collectives: 42 us -> none  [body(): maps = lax.all_gather(coarse_map[0], 'sub', axis=0, tiled=True)]
    pallas_call x18 -> x19, Pallas kernels: 76.7 us -> 45.9 us  [call(): pl.pallas_call(kernel, name=name, out_shape=tuple(outs), in_specs=[specs....]
    unnamed x83 -> x16, local copies, waits for them, and re-layouts: 26.5 us -> 9.73 us
    all_to_all x1, waiting for transfers between devices: 0.01 us -> 13.4 us  [body(): mine_rows = lax.all_to_all(picked, 'sub', 0, 0, tiled=True)]
    ppermute x32, waiting for transfers between devices: 50.3 us -> 38.3 us  [the longest x28 35.8 us: exchange(): return [lax.ppermute(out, 'sub', swap) for out, swap in zip(outs, swaps)]]
    all_to_all x2 -> x3, blocking collectives: 36.8 us -> 45 us  [the longest x2 34.8 us: share(): lax.all_to_all(send, 'sub', 0, 0, tiled=True, axis_index_groups=cores)]
    all_to_all x1, waiting for transfers between devices: 8.06 us -> 11.1 us  [share(): lax.all_to_all(send, 'sub', 0, 0, tiled=True, axis_index_groups=cores)]
  transfers between devices with their start and end apart: 35 -> 35, of which waited for: 23 -> 20; matrix products, arithmetic and copies ran while one was open for 1% -> 0% of each run, Pallas kernels for 5% -> 5%
where the time goes in v2:
time: 216 us; the launch traced here: 215 us
  waiting for transfers between devices  62.8 us (29%)
  starting transfers between devices  48.3 us (22%)
  Pallas kernels  45.9 us (21%)
  blocking collectives  45 us (21%)
  local copies, waits for them, and re-layouts  11.3 us (5%)
    pallas_call x19, Pallas kernels, call(): pl.pallas_call(kernel, name=name, out_shape=tuple(outs), in_specs=[specs....  45.9 us
    ppermute x28, starting transfers between devices, exchange(): return [lax.ppermute(out, 'sub', swap) for out, swap in zip(outs, swaps)]  37.6 us
    ppermute x28, waiting for transfers between devices, exchange(): return [lax.ppermute(out, 'sub', swap) for out, swap in zip(outs, swaps)]  35.8 us
    all_to_all x2, blocking collectives, share(): lax.all_to_all(send, 'sub', 0, 0, tiled=True, axis_index_groups=cores)  34.8 us
    all_to_all x1, waiting for transfers between devices, body(): mine_rows = lax.all_to_all(picked, 'sub', 0, 0, tiled=True)  13.4 us
    all_to_all x1, waiting for transfers between devices, share(): lax.all_to_all(send, 'sub', 0, 0, tiled=True, axis_index_groups=cores)  11.1 us
    all_to_all x1, blocking collectives, body(): maps = lax.all_to_all(maps, 'sub', 0, 0, tiled=True)  10.3 us
    unnamed x16, local copies, waits for them, and re-layouts  9.73 us
  transfers between devices with their start and end apart: 35, of which 20 were waited for; matrix products, arithmetic and copies ran while one was open for 0% of the time, Pallas kernels for 5%

profile of v2, /device:TPU:0, one launch (start us, length us, event | category | flops | bytes accessed | tf_op | source)
XLA Modules:
  0.0 215.1 jit_solution(6573945433254881558)
XLA Ops:
  4.6 5.1 %collective-permute-start = (f32[256,128]{1,0:T(8,128)S(1)}, f32[256,128]{1,0:T(8,128)S(1)}, u32[]{:S(2)}, u32[]{:S(2)}) collective-permute-start(f32[256,128]{1,0:T(8,128)S(1)} %get-tuple-element.84), channel_id=1, source_target_pairs={{0,24},{1,25},{2,26},{3,27},{4,28},{5,29},{6,30},{7,31},{8,16},{9,... | collective-permute-start | bytes 393224 | tf_op jit(solution)/shard_map/ppermute | solution.py:444
  13.5 10.3 %all_to_all.64 = s32[32,1,128]{2,1,0:T(1,128)S(1)} all-to-all(s32[32,1,128]{2,1,0:T(1,128)S(1)} %broadcast_in_dim.11), channel_id=1, replica_groups=mesh['sub'=32] {'sub'}, dimensions={0} | all-to-all | bytes 32768 | tf_op jit(solution)/shard_map/all_to_all | solution.py:479
  25.4 3.7 %coarse_columns.1 = f32[1536,128]{1,0:T(8,128)} custom-call(s32[32,128]{1,0:T(8,128)S(1)} %bitcast.49, f32[128,4096]{1,0:T(8,128)S(1)} %copy-done.6), custom_call_target="tpu_custom_call" | custom-call | bytes 8388608 | tf_op jit(solution)/shard_map/coarse_columns/pallas_call | solution.py:43
  34.1 4.8 %residual_and_terms.1 = (f32[1536,128]{1,0:T(8,128)}, f32[1536,128]{1,0:T(8,128)}, f32[896,128]{1,0:T(8,128)}) custom-call(f32[1536,128]{1,0:T(8,128)S(1)} %bitcast.40, f32[256,128]{1,0:T(8,128)S(1)} %collective-permute-done.a0, f32[256,128]{1,0:T(8,128)S(1)} %collective-permute-done.1.a1, f32[256,128]{1,0:T(8,128)S(1)} %collective-permute-done.2.a2, ...), custom_call_target="tpu_custom_call" | custom-call | bytes 8388608 | tf_op jit(solution)/shard_map/residual_and_terms/pallas_call | solution.py:43
  38.9 13.4 %all-to-all-done.2 = f32[32,48,128]{2,1,0:T(8,128)S(1)} async-done(((f32[32,48,128]{2,1,0:T(8,128)}), f32[32,48,128]{2,1,0:T(8,128)S(1)}, u32[]{:S(2)}, u32[]{:S(2)}) %all-to-all-start.2) | async-done | bytes 786464 | tf_op jit(solution)/shard_map/all_to_all | solution.py:491
  52.3 4.6 %all-to-all-start.1 = ((f32[16,56,128]{2,1,0:T(8,128)}), f32[16,56,128]{2,1,0:T(8,128)S(1)}, u32[]{:S(2)}, u32[]{:S(2)}) async-start(f32[16,56,128]{2,1,0:T(8,128)} %bitcast.12), calls=%async_computation.1 | async-start | bytes 917504 | tf_op jit(solution)/shard_map/all_to_all | solution.py:525
  59.9 11.1 %all-to-all-done.1 = f32[16,56,128]{2,1,0:T(8,128)S(1)} async-done(((f32[16,56,128]{2,1,0:T(8,128)}), f32[16,56,128]{2,1,0:T(8,128)S(1)}, u32[]{:S(2)}, u32[]{:S(2)}) %all-to-all-start.1) | async-done | bytes 458784 | tf_op jit(solution)/shard_map/all_to_all | solution.py:525
  87.1 3.3 %operator.2 = (f32[1536,128]{1,0:T(8,128)S(1)}, f32[1536,128]{1,0:T(8,128)S(1)}, f32[256,128]{1,0:T(8,128)S(1)}, f32[256,128]{1,0:T(8,128)S(1)}, f32[256,128]{1,0:T(8,128)S(1)}, /*index=5*/f32[256,128]{1,0:T(8,128)S(1)}) custom-call(f32[1536,128]{1,0:T(8,128)S(1)} %get-tuple-element.104.part_ref, f32[256,128]{1,0:T(8,128)S(1)} %collective-permute-done.6.a0, ...), custom_call_target="tpu_custom_call" | custom-call | bytes 8388608 | tf_op jit(solution)/shard_map/operator/pallas_call | solution.py:43
  94.2 3.9 %collective-permute-done.10.a0 = f32[256,128]{1,0:T(8,128)S(1)} collective-permute-done((f32[256,128]{1,0:T(8,128)S(1)}, f32[256,128]{1,0:T(8,128)S(1)}, u32[]{:S(2)}, u32[]{:S(2)}) %collective-permute-start.10) | collective-permute-done | bytes 131104 | tf_op jit(solution)/shard_map/ppermute | solution.py:444
  101.1 4.5 %start.1 = (f32[1536,128]{1,0:T(8,128)S(1)}, f32[1536,128]{1,0:T(8,128)S(1)}, f32[896,128]{1,0:T(8,128)S(1)}) custom-call(f32[1536,128]{1,0:T(8,128)S(1)} %get-tuple-element.111.part_ref, f32[256,128]{1,0:T(8,128)S(1)} %collective-permute-done.10.a0, f32[256,128]{1,0:T(8,128)S(1)} %collective-permute-done.11.a1, f32[256,128]{1,0:T(8,128)S(1)} %collective-permute-done.12.a2, ...), custom_call_target="tpu_custom_call" | custom-call | bytes 8388608 | tf_op jit(solution)/shard_map/start/pallas_call | solution.py:43
  105.7 17.3 %all_to_all.65 = f32[16,56,128]{2,1,0:T(8,128)S(1)} all-to-all(f32[16,56,128]{2,1,0:T(8,128)S(1)} %bitcast.48), channel_id=1, replica_groups={{0,2,4,6,8,10,12,14,16,18,20,22,24,26,28,30},{1,3,5,7,9,11,13,15,17,19,..., dimensions={0} | all-to-all | bytes 917504 | tf_op jit(solution)/shard_map/all_to_all | solution.py:525
  130.6 3.3 %collective-permute-done.15.a0 = f32[256,128]{1,0:T(8,128)S(1)} collective-permute-done((f32[256,128]{1,0:T(8,128)S(1)}, f32[256,128]{1,0:T(8,128)S(1)}, u32[]{:S(2)}, u32[]{:S(2)}) %collective-permute-start.15) | collective-permute-done | bytes 131104 | tf_op jit(solution)/shard_map/ppermute | solution.py:444
  134.0 3.1 %collective-permute-done.16.a1 = f32[256,128]{1,0:T(8,128)S(1)} collective-permute-done((f32[256,128]{1,0:T(8,128)S(1)}, f32[256,128]{1,0:T(8,128)S(1)}, u32[]{:S(2)}, u32[]{:S(2)}) %collective-permute-start.16) | collective-permute-done | bytes 131104 | tf_op jit(solution)/shard_map/ppermute | solution.py:444
  137.5 3.3 %operator.3 = (f32[1536,128]{1,0:T(8,128)S(1)}, f32[1536,128]{1,0:T(8,128)S(1)}, f32[256,128]{1,0:T(8,128)S(1)}, f32[256,128]{1,0:T(8,128)S(1)}, f32[256,128]{1,0:T(8,128)S(1)}, /*index=5*/f32[256,128]{1,0:T(8,128)S(1)}) custom-call(f32[1536,128]{1,0:T(8,128)S(1)} %get-tuple-element.124.part_ref, f32[256,128]{1,0:T(8,128)S(1)} %collective-permute-done.15.a0, ...), custom_call_target="tpu_custom_call" | custom-call | bytes 8388608 | tf_op jit(solution)/shard_map/operator/pallas_call | solution.py:43
  145.4 3.1 %collective-permute-done.19.a0 = f32[256,128]{1,0:T(8,128)S(1)} collective-permute-done((f32[256,128]{1,0:T(8,128)S(1)}, f32[256,128]{1,0:T(8,128)S(1)}, u32[]{:S(2)}, u32[]{:S(2)}) %collective-permute-start.19) | collective-permute-done | bytes 131104 | tf_op jit(solution)/shard_map/ppermute | solution.py:444
  148.5 3.6 %collective-permute-done.20.a1 = f32[256,128]{1,0:T(8,128)S(1)} collective-permute-done((f32[256,128]{1,0:T(8,128)S(1)}, f32[256,128]{1,0:T(8,128)S(1)}, u32[]{:S(2)}, u32[]{:S(2)}) %collective-permute-start.20) | collective-permute-done | bytes 131104 | tf_op jit(solution)/shard_map/ppermute | solution.py:444
  152.0 4.7 %first_update.1 = (f32[1536,128]{1,0:T(8,128)S(1)}, f32[1536,128]{1,0:T(8,128)S(1)}, f32[1536,128]{1,0:T(8,128)S(1)}, f32[1536,128]{1,0:T(8,128)S(1)}, f32[1536,...) custom-call(f32[1536,128]{1,0:T(8,128)S(1)} %get-tuple-element.129.part_ref, ...), custom_call_target="tpu_custom_call" | custom-call | bytes 8388608 | tf_op jit(solution)/shard_map/first_update/pallas_call | solution.py:43
  156.7 17.4 %all_to_all.66 = f32[16,56,128]{2,1,0:T(8,128)S(1)} all-to-all(f32[16,56,128]{2,1,0:T(8,128)S(1)} %bitcast.47), channel_id=1, replica_groups={{0,2,4,6,8,10,12,14,16,18,20,22,24,26,28,30},{1,3,5,7,9,11,13,15,17,19,..., dimensions={0} | all-to-all | bytes 917504 | tf_op jit(solution)/shard_map/all_to_all | solution.py:525
  181.8 3.2 %collective-permute-done.24.a0 = f32[256,128]{1,0:T(8,128)S(1)} collective-permute-done((f32[256,128]{1,0:T(8,128)S(1)}, f32[256,128]{1,0:T(8,128)S(1)}, u32[]{:S(2)}, u32[]{:S(2)}) %collective-permute-start.24) | collective-permute-done | bytes 131104 | tf_op jit(solution)/shard_map/ppermute | solution.py:444
  188.6 4.9 %second_update.1 = (f32[256,128]{1,0:T(8,128)S(1)}, f32[256,128]{1,0:T(8,128)S(1)}, f32[256,128]{1,0:T(8,128)S(1)}, f32[256,128]{1,0:T(8,128)S(1)}, f32[256,128]...) custom-call(f32[1536,128]{1,0:T(8,128)S(1)} %get-tuple-element.141.p, ...), custom_call_target="tpu_custom_call" | custom-call | bytes 8388608 | tf_op jit(solution)/shard_map/second_update/pallas_call | solution.py:43
  193.5 3.2 %all-to-all-start.5 = ((f32[32,8,128]{2,1,0:T(8,128)}), f32[32,8,128]{2,1,0:T(8,128)S(1)}, u32[]{:S(2)}, u32[]{:S(2)}) async-start(f32[32,8,128]{2,1,0:T(8,128)} %bitcast.22), calls=%async_computation.5 | async-start | bytes 262144 | tf_op jit(solution)/shard_map/all_to_all | solution.py:614
  196.7 3.7 %collective-permute-start.28 = (f32[256,128]{1,0:T(8,128)S(1)}, f32[256,128]{1,0:T(8,128)S(1)}, u32[]{:S(2)}, u32[]{:S(2)}) collective-permute-start(f32[256,128]{1,0:T(8,128)S(1)} %get-tuple-element.154), channel_id=1, source_target_pairs={{0,24},{1,25},{2,26},{3,27},{4,28},{5,29},{6,30},{7,31},{8,16},{9,... | collective-permute-start | bytes 393224 | tf_op jit(solution)/shard_map/ppermute | solution.py:444
  206.8 3.7 %collective-permute-done.29.a1 = f32[256,128]{1,0:T(8,128)S(1)} collective-permute-done((f32[256,128]{1,0:T(8,128)S(1)}, f32[256,128]{1,0:T(8,128)S(1)}, u32[]{:S(2)}, u32[]{:S(2)}) %collective-permute-start.29) | collective-permute-done | bytes 131104 | tf_op jit(solution)/shard_map/ppermute | solution.py:444
  210.6 4.5 %last_update.1 = (f32[1536,128]{1,0:T(8,128)}, f32[1536,128]{1,0:T(8,128)}) custom-call(s32[1,1024]{1,0:T(1,128)S(1)} %bitcast.55, f32[8,128]{1,0:T(8,128)S(1)} %get-tuple-element.152.state_ref, f32[256,128]{1,0:T(8,128)S(1)} %bitcast.46, f32[256,128]{1,0:T(8,128)S(1)} %collective-permute-done.28.a0, f32[256,128]{1,0:T(8,128)S(1)} %collective-permute-done.29.a1, ...), custom_call_target="tpu_custom_call" | custom-call | bytes 8388608 | tf_op jit(solution)/shard_map/last_update/pallas_call | solution.py:43
  (92 shorter events, 70.4 us)
Async XLA Ops:
  4.6 19.1 %collective-permute-start = (f32[256,128]{1,0:T(8,128)S(1)}, f32[256,128]{1,0:T(8,128)S(1)}, u32[]{:S(2)}, u32[]{:S(2)}) collective-permute-start(f32[256,128]{1,0:T(8,128)S(1)} %get-tuple-element.84), channel_id=1, source_target_pairs={{0,24},{1,25},{2,26},{3,27},{4,28},{5,29},{6,30},{7,31},{8,16},{9,... | collective-permute-start | bytes 393224 | tf_op jit(solution)/shard_map/ppermute | solution.py:444
  9.7 14.0 %collective-permute-start.1 = (f32[256,128]{1,0:T(8,128)S(1)}, f32[256,128]{1,0:T(8,128)S(1)}, u32[]{:S(2)}, u32[]{:S(2)}) collective-permute-start(f32[256,128]{1,0:T(8,128)S(1)} %get-tuple-element.85), channel_id=1, source_target_pairs={{0,31},{1,2},{2,1},{3,4},{4,3},{5,6},{6,5},{7,8},{8,7},{9,10},{10,... | collective-permute-start | bytes 393224 | tf_op jit(solution)/shard_map/ppermute | solution.py:444
  11.1 12.6 %collective-permute-start.2 = (f32[256,128]{1,0:T(8,128)S(1)}, f32[256,128]{1,0:T(8,128)S(1)}, u32[]{:S(2)}, u32[]{:S(2)}) collective-permute-start(f32[256,128]{1,0:T(8,128)S(1)} %get-tuple-element.86), channel_id=1, source_target_pairs={{0,8},{1,9},{2,10},{3,11},{4,12},{5,13},{6,14},{7,15},{8,0},{9,1},... | collective-permute-start | bytes 393224 | tf_op jit(solution)/shard_map/ppermute | solution.py:444
  12.8 11.0 %collective-permute-start.3 = (f32[256,128]{1,0:T(8,128)S(1)}, f32[256,128]{1,0:T(8,128)S(1)}, u32[]{:S(2)}, u32[]{:S(2)}) collective-permute-start(f32[256,128]{1,0:T(8,128)S(1)} %get-tuple-element.87), channel_id=1, source_target_pairs={{0,1},{1,0},{2,3},{3,2},{4,5},{5,4},{6,7},{7,6},{8,9},{9,8},{10,11... | collective-permute-start | bytes 393224 | tf_op jit(solution)/shard_map/ppermute | solution.py:444
  29.1 23.2 %all-to-all-start.2 = ((f32[32,48,128]{2,1,0:T(8,128)}), f32[32,48,128]{2,1,0:T(8,128)S(1)}, u32[]{:S(2)}, u32[]{:S(2)}) async-start(f32[32,48,128]{2,1,0:T(8,128)} %bitcast.15), calls=%async_computation.2 | async-start | bytes 1572864 | tf_op jit(solution)/shard_map/all_to_all | solution.py:491
  52.3 18.7 %all-to-all-start.1 = ((f32[16,56,128]{2,1,0:T(8,128)}), f32[16,56,128]{2,1,0:T(8,128)S(1)}, u32[]{:S(2)}, u32[]{:S(2)}) async-start(f32[16,56,128]{2,1,0:T(8,128)} %bitcast.12), calls=%async_computation.1 | async-start | bytes 917504 | tf_op jit(solution)/shard_map/all_to_all | solution.py:525
  59.8 11.2 %collective-permute-start.4 = (f32[48,768]{1,0:T(8,128)S(1)}, f32[48,768]{1,0:T(8,128)S(1)}, u32[]{:S(2)}, u32[]{:S(2)}) collective-permute-start(f32[48,768]{1,0:T(8,128)S(1)} %get-tuple-element.95), channel_id=1, source_target_pairs={{0,1},{1,0},{2,3},{3,2},{4,5},{5,4},{6,7},{7,6},{8,9},{9,8},{10,11... | collective-permute-start | bytes 442376 | tf_op jit(solution)/shard_map/ppermute | solution.py:522
  75.3 10.1 %collective-permute-start.6 = (f32[256,128]{1,0:T(8,128)S(1)}, f32[256,128]{1,0:T(8,128)S(1)}, u32[]{:S(2)}, u32[]{:S(2)}) collective-permute-start(f32[256,128]{1,0:T(8,128)S(1)} %get-tuple-element.105), channel_id=1, source_target_pairs={{0,24},{1,25},{2,26},{3,27},{4,28},{5,29},{6,30},{7,31},{8,16},{9,... | collective-permute-start | bytes 393224 | tf_op jit(solution)/shard_map/ppermute | solution.py:444
  76.8 9.2 %collective-permute-start.7 = (f32[256,128]{1,0:T(8,128)S(1)}, f32[256,128]{1,0:T(8,128)S(1)}, u32[]{:S(2)}, u32[]{:S(2)}) collective-permute-start(f32[256,128]{1,0:T(8,128)S(1)} %get-tuple-element.106), channel_id=1, source_target_pairs={{0,31},{1,2},{2,1},{3,4},{4,3},{5,6},{6,5},{7,8},{8,7},{9,10},{10,... | collective-permute-start | bytes 393224 | tf_op jit(solution)/shard_map/ppermute | solution.py:444
  79.2 8.0 %collective-permute-start.8 = (f32[256,128]{1,0:T(8,128)S(1)}, f32[256,128]{1,0:T(8,128)S(1)}, u32[]{:S(2)}, u32[]{:S(2)}) collective-permute-start(f32[256,128]{1,0:T(8,128)S(1)} %get-tuple-element.107), channel_id=1, source_target_pairs={{0,8},{1,9},{2,10},{3,11},{4,12},{5,13},{6,14},{7,15},{8,0},{9,1},... | collective-permute-start | bytes 393224 | tf_op jit(solution)/shard_map/ppermute | solution.py:444
  79.4 7.7 %collective-permute-start.9 = (f32[256,128]{1,0:T(8,128)S(1)}, f32[256,128]{1,0:T(8,128)S(1)}, u32[]{:S(2)}, u32[]{:S(2)}) collective-permute-start(f32[256,128]{1,0:T(8,128)S(1)} %get-tuple-element.108), channel_id=1, source_target_pairs={{0,1},{1,0},{2,3},{3,2},{4,5},{5,4},{6,7},{7,6},{8,9},{9,8},{10,11... | collective-permute-start | bytes 393224 | tf_op jit(solution)/shard_map/ppermute | solution.py:444
  90.5 7.6 %collective-permute-start.10 = (f32[256,128]{1,0:T(8,128)S(1)}, f32[256,128]{1,0:T(8,128)S(1)}, u32[]{:S(2)}, u32[]{:S(2)}) collective-permute-start(f32[256,128]{1,0:T(8,128)S(1)} %get-tuple-element.112), channel_id=1, source_target_pairs={{0,24},{1,25},{2,26},{3,27},{4,28},{5,29},{6,30},{7,31},{8,16},{9,... | collective-permute-start | bytes 393224 | tf_op jit(solution)/shard_map/ppermute | solution.py:444
  92.2 8.9 %collective-permute-start.11 = (f32[256,128]{1,0:T(8,128)S(1)}, f32[256,128]{1,0:T(8,128)S(1)}, u32[]{:S(2)}, u32[]{:S(2)}) collective-permute-start(f32[256,128]{1,0:T(8,128)S(1)} %get-tuple-element.113), channel_id=1, source_target_pairs={{0,31},{1,2},{2,1},{3,4},{4,3},{5,6},{6,5},{7,8},{8,7},{9,10},{10,... | collective-permute-start | bytes 393224 | tf_op jit(solution)/shard_map/ppermute | solution.py:444
  125.7 8.3 %collective-permute-start.15 = (f32[256,128]{1,0:T(8,128)S(1)}, f32[256,128]{1,0:T(8,128)S(1)}, u32[]{:S(2)}, u32[]{:S(2)}) collective-permute-start(f32[256,128]{1,0:T(8,128)S(1)} %get-tuple-element.125), channel_id=1, source_target_pairs={{0,24},{1,25},{2,26},{3,27},{4,28},{5,29},{6,30},{7,31},{8,16},{9,... | collective-permute-start | bytes 393224 | tf_op jit(solution)/shard_map/ppermute | solution.py:444
  128.2 8.9 %collective-permute-start.16 = (f32[256,128]{1,0:T(8,128)S(1)}, f32[256,128]{1,0:T(8,128)S(1)}, u32[]{:S(2)}, u32[]{:S(2)}) collective-permute-start(f32[256,128]{1,0:T(8,128)S(1)} %get-tuple-element.126), channel_id=1, source_target_pairs={{0,31},{1,2},{2,1},{3,4},{4,3},{5,6},{6,5},{7,8},{8,7},{9,10},{10,... | collective-permute-start | bytes 393224 | tf_op jit(solution)/shard_map/ppermute | solution.py:444
  140.8 7.6 %collective-permute-start.19 = (f32[256,128]{1,0:T(8,128)S(1)}, f32[256,128]{1,0:T(8,128)S(1)}, u32[]{:S(2)}, u32[]{:S(2)}) collective-permute-start(f32[256,128]{1,0:T(8,128)S(1)} %get-tuple-element.130), channel_id=1, source_target_pairs={{0,24},{1,25},{2,26},{3,27},{4,28},{5,29},{6,30},{7,31},{8,16},{9,... | collective-permute-start | bytes 393224 | tf_op jit(solution)/shard_map/ppermute | solution.py:444
  143.3 8.8 %collective-permute-start.20 = (f32[256,128]{1,0:T(8,128)S(1)}, f32[256,128]{1,0:T(8,128)S(1)}, u32[]{:S(2)}, u32[]{:S(2)}) collective-permute-start(f32[256,128]{1,0:T(8,128)S(1)} %get-tuple-element.131), channel_id=1, source_target_pairs={{0,31},{1,2},{2,1},{3,4},{4,3},{5,6},{6,5},{7,8},{8,7},{9,10},{10,... | collective-permute-start | bytes 393224 | tf_op jit(solution)/shard_map/ppermute | solution.py:444
  176.8 8.3 %collective-permute-start.24 = (f32[256,128]{1,0:T(8,128)S(1)}, f32[256,128]{1,0:T(8,128)S(1)}, u32[]{:S(2)}, u32[]{:S(2)}) collective-permute-start(f32[256,128]{1,0:T(8,128)S(1)} %get-tuple-element.142), channel_id=1, source_target_pairs={{0,24},{1,25},{2,26},{3,27},{4,28},{5,29},{6,30},{7,31},{8,16},{9,... | collective-permute-start | bytes 393224 | tf_op jit(solution)/shard_map/ppermute | solution.py:444
  179.1 8.9 %collective-permute-start.25 = (f32[256,128]{1,0:T(8,128)S(1)}, f32[256,128]{1,0:T(8,128)S(1)}, u32[]{:S(2)}, u32[]{:S(2)}) collective-permute-start(f32[256,128]{1,0:T(8,128)S(1)} %get-tuple-element.143), channel_id=1, source_target_pairs={{0,31},{1,2},{2,1},{3,4},{4,3},{5,6},{6,5},{7,8},{8,7},{9,10},{10,... | collective-permute-start | bytes 393224 | tf_op jit(solution)/shard_map/ppermute | solution.py:444
  181.0 7.6 %collective-permute-start.26 = (f32[256,128]{1,0:T(8,128)S(1)}, f32[256,128]{1,0:T(8,128)S(1)}, u32[]{:S(2)}, u32[]{:S(2)}) collective-permute-start(f32[256,128]{1,0:T(8,128)S(1)} %get-tuple-element.144), channel_id=1, source_target_pairs={{0,8},{1,9},{2,10},{3,11},{4,12},{5,13},{6,14},{7,15},{8,0},{9,1},... | collective-permute-start | bytes 393224 | tf_op jit(solution)/shard_map/ppermute | solution.py:444
  193.5 17.2 %all-to-all-start.5 = ((f32[32,8,128]{2,1,0:T(8,128)}), f32[32,8,128]{2,1,0:T(8,128)S(1)}, u32[]{:S(2)}, u32[]{:S(2)}) async-start(f32[32,8,128]{2,1,0:T(8,128)} %bitcast.22), calls=%async_computation.5 | async-start | bytes 262144 | tf_op jit(solution)/shard_map/all_to_all | solution.py:614
  196.7 10.1 %collective-permute-start.28 = (f32[256,128]{1,0:T(8,128)S(1)}, f32[256,128]{1,0:T(8,128)S(1)}, u32[]{:S(2)}, u32[]{:S(2)}) collective-permute-start(f32[256,128]{1,0:T(8,128)S(1)} %get-tuple-element.154), channel_id=1, source_target_pairs={{0,24},{1,25},{2,26},{3,27},{4,28},{5,29},{6,30},{7,31},{8,16},{9,... | collective-permute-start | bytes 393224 | tf_op jit(solution)/shard_map/ppermute | solution.py:444
  200.4 10.1 %collective-permute-start.29 = (f32[256,128]{1,0:T(8,128)S(1)}, f32[256,128]{1,0:T(8,128)S(1)}, u32[]{:S(2)}, u32[]{:S(2)}) collective-permute-start(f32[256,128]{1,0:T(8,128)S(1)} %get-tuple-element.155), channel_id=1, source_target_pairs={{0,31},{1,2},{2,1},{3,4},{4,3},{5,6},{6,5},{7,8},{8,7},{9,10},{10,... | collective-permute-start | bytes 393224 | tf_op jit(solution)/shard_map/ppermute | solution.py:444
  202.1 8.5 %collective-permute-start.30 = (f32[256,128]{1,0:T(8,128)S(1)}, f32[256,128]{1,0:T(8,128)S(1)}, u32[]{:S(2)}, u32[]{:S(2)}) collective-permute-start(f32[256,128]{1,0:T(8,128)S(1)} %get-tuple-element.156), channel_id=1, source_target_pairs={{0,8},{1,9},{2,10},{3,11},{4,12},{5,13},{6,14},{7,15},{8,0},{9,1},... | collective-permute-start | bytes 393224 | tf_op jit(solution)/shard_map/ppermute | solution.py:444
  (19 other events, 156.5 us)
